TPU v7x, 256 devices: a whole 4x4x8 slice. The times are simulated.
256 devices in a mesh: tm: 8 (over x, core), height: 4 (over y), dp: 8 (over z).
Axes of the slice: x: 4, y: 4, z: 8, core: 2. Of those that a mesh axis runs over, the one named last changes fastest.
Arguments:
- activations: bfloat16 [8, 16, 4, 256, 256], P('dp', 'tm', 'height'), may hold values from -9 to 9
- cotangent: bfloat16 [8, 16, 4, 256, 256], P('dp', 'tm', 'height'), may hold values from -9 to 9
- clip_frames: int32 [8], P('dp'), may hold values from 15 to 16, as said below
- conv_weight: bfloat16 [256, 27, 256], P('dp'), may hold values from -0.078125 to 0.078125
- group_centre: float32 [8, 32], P('dp'), may hold values from -3 to 3
- group_scale: float32 [8, 32], P('dp'), may hold values from 0.5 to 2
- norm_gain: float32 [256], replicated, may hold values from 0.5 to 1.5
- norm_bias: float32 [256], replicated, may hold values from -0.5 to 0.5
Outputs:
- grad_input: bfloat16 [8, 16, 4, 256, 256], P('dp', 'tm', 'height')
- weight_grad: bfloat16 [6912, 256], P(('tm', 'height', 'dp'))
Inputs may be any that keep to these rules, and one draw needn't show every extreme that they name: `clip_frames`: some clip has exactly 16 frames and another exactly 15 in every draw.
All inputs are finite; a program needn't handle non-finite values.
Results may differ from a plain program's by a relative error of at most 0.0031.
Values may be sent and summed in bfloat16 or wider, within the bound.
A program may use at most 64 MiB of HBM per device.

v0:
```python
import jax
import jax.numpy as jnp
from jax import lax
from jax.sharding import PartitionSpec as P


def passed_along(block, axis, distance):
    devices = range(lax.axis_size(axis))
    route = [(i - distance, i) for i in devices if i - distance in devices]
    return lax.ppermute(block, axis, route)


def padded_2(cells, sides, width):
    for axis, dim in sides:
        count = lax.axis_size(axis)
        ends = count - 1
        head = lax.slice_in_dim(cells, 0, width, axis=dim)
        tail = lax.slice_in_dim(cells, cells.shape[dim] - width, cells.shape[dim], axis=dim)
        cells = jnp.concatenate(
            [
                lax.ppermute(tail, axis, [(i, (i + 1) % count) for i in range(ends)]),
                cells,
                lax.ppermute(head, axis, [((i + 1) % count, i) for i in range(ends)]),
            ],
            axis=dim,
        )
    return cells


def contract_inner(matrix, operand):
    return lax.dot_general(
        matrix, operand, (((1,), (1,)), ((), ())), preferred_element_type=jnp.float32
    )


def contract_rows(matrix, operand):
    return lax.dot_general(
        matrix, operand, (((0,), (0,)), ((), ())), preferred_element_type=jnp.float32
    )


def per_device(
    activations,
    cotangent,
    clip_frames,
    conv_weight,
    group_centre,
    group_scale,
    norm_gain,
    norm_bias,
):
    slab_acts = activations[0]
    slab_cot = cotangent[0]
    slab_len, row_count, col_count, channels = slab_acts.shape
    group_count = group_centre.shape[1]
    per_group = channels // group_count
    tap_count = conv_weight.shape[1]
    clip_len = clip_frames[0]
    centre = group_centre[0]
    spread = group_scale[0]
    first_frame = lax.axis_index("tm") * slab_len
    validity = (first_frame + jnp.arange(slab_len) < clip_len).astype(jnp.float32)[
        :, None, None, None
    ]
    grouped = slab_acts.astype(jnp.float32).reshape(
        slab_len, row_count, col_count, group_count, per_group
    )
    normed = ((grouped - centre[:, None]) * spread[:, None]).reshape(
        slab_len, row_count, col_count, channels
    )
    shifted = normed * norm_gain + norm_bias
    sigmoid_val = jax.nn.sigmoid(shifted)
    conv_input = (shifted * sigmoid_val * validity).astype(jnp.bfloat16)
    masked = slab_cot * validity.astype(jnp.bfloat16)
    following = passed_along(masked, "tm", -1)
    extended = jnp.concatenate([masked, following], axis=0)
    banded = padded_2(extended, (("height", 1),), 1)
    padded = jnp.pad(banded, ((0, 0), (0, 0), (1, 1), (0, 0)))
    cell_count = slab_len * row_count * col_count

    def window(tap_idx):
        tap_t, tap_h, tap_w = (tap_idx // 9, tap_idx // 3 % 3, tap_idx % 3)
        region = padded[
            2 - tap_t : 2 - tap_t + slab_len,
            2 - tap_h : 2 - tap_h + row_count,
            2 - tap_w : 2 - tap_w + col_count,
        ]
        return region.reshape(cell_count, channels)

    shard_rows = lax.all_gather(conv_weight, "dp", axis=0, tiled=True)
    summed = jnp.zeros((cell_count, shard_rows.shape[0]), jnp.float32)
    for input_tap_idx in range(tap_count):
        summed = summed + contract_inner(window(input_tap_idx), shard_rows[:, input_tap_idx, :])
    input_grad = summed.reshape(slab_len, row_count, col_count, shard_rows.shape[0])
    derivative = sigmoid_val * (1.0 + shifted * (1.0 - sigmoid_val))
    upstream = input_grad * derivative * validity * norm_gain
    up_grouped = upstream.reshape(-1, group_count, per_group)
    normed_grouped = normed.reshape(-1, group_count, per_group)
    local_first = jnp.sum(up_grouped, axis=(0, 2))
    local_second = jnp.sum(up_grouped * normed_grouped, axis=(0, 2))
    first_sum, second_sum = lax.psum((local_first, local_second), ("tm", "height"))
    population = clip_len.astype(jnp.float32) * (
        row_count * lax.axis_size("height") * col_count * per_group
    )
    correction = (first_sum / population)[:, None] + normed_grouped * (second_sum / population)[
        :, None
    ]
    grad_flat = spread[:, None] * (up_grouped - correction)
    grad_input = (grad_flat.reshape(slab_len, row_count, col_count, channels) * validity).astype(
        jnp.bfloat16
    )
    flat_input = conv_input.reshape(cell_count, channels)
    all_devices = lax.axis_size("tm") * lax.axis_size("height") * lax.axis_size("dp")
    inv_cells = 1.0 / (cell_count * all_devices)
    total_rows = channels * tap_count
    per_tap = [contract_rows(flat_input, window(tap_idx)) for tap_idx in range(tap_count)]
    full_term = (jnp.stack(per_tap, axis=1) * inv_cells).reshape(total_rows, channels)
    weight_grad = lax.psum_scatter(
        full_term, ("tm", "height", "dp"), scatter_dimension=0, tiled=True
    )
    return (grad_input[None], weight_grad.astype(jnp.bfloat16))


def solution(mesh):
    return jax.shard_map(
        per_device,
        mesh=mesh,
        in_specs=(
            P("dp", "tm", "height", None, None),
            P("dp", "tm", "height", None, None),
            P("dp"),
            P("dp", None, None),
            P("dp", None),
            P("dp", None),
            P(),
            P(),
        ),
        out_specs=(P("dp", "tm", "height", None, None), P(("tm", "height", "dp"), None)),
        check_vma=False,
    )
```

profile of v0, /device:TPU:1, one launch (start us, length us, event | category | flops | bytes accessed | tf_op | source)
XLA Modules:
  0.0 1134.7 jit_solution(18050656002491248416)
XLA Ops:
  8.9 5.1 collective-permute-start
  14.1 3.4 collective-permute-done
  17.6 3.2 collective-permute-start.1
  24.9 4.4 collective-permute-done.1
  29.3 4.1 collective-permute-done.2
  46.2 7.7 copy.95
  53.8 8.5 mul.392
  62.4 636.0 %fusion = f32[32,256]{1,0:T(8,128)S(1)} fusion(f32[6912,256]{1,0:T(8,128)} %mul.392), kind=kCustom, calls=%all-reduce-scatter | all-reduce-scatter fusion | flops 2097153 | bytes 7110656
  699.0 68.4 %collective-permute-start.10 = (bf16[32,256]{1,0:T(8,128)(2,1)}, bf16[32,256]{1,0:T(8,128)(2,1)S(1)}, u32[]{:S(2)}, u32[]{:S(2)}) collective-permute-start(bf16[32,256]{1,0:T(8,128)(2,1)} %convert.79), channel_id=1, source_target_pairs={{0,8},{1,9},{2,10},{3,11},{4,12},{5,13},{6,14},{7,15},{8,16},{9,17... | collective-permute-start | bytes 49160
  767.4 4.4 collective-permute-start.11
  771.8 5.5 collective-permute-start.12
  777.3 5.8 collective-permute-start.13
  783.1 3.7 collective-permute-start.42
  787.7 5.3 collective-permute-start.14
  792.9 7.5 collective-permute-start.15
  800.5 8.2 collective-permute-start.16
  808.6 2.1 collective-permute-start.17
  810.8 5.6 collective-permute-start.18
  816.4 2.5 collective-permute-start.19
  819.0 3.3 collective-permute-start.20
  822.2 5.9 collective-permute-start.21
  828.1 6.0 collective-permute-start.22
  834.2 7.1 collective-permute-start.23
  841.3 4.0 collective-permute-start.24
  849.2 2.1 collective-permute-start.27
  851.4 2.2 collective-permute-start.28
  853.6 2.5 collective-permute-start.29
  856.2 7.3 collective-permute-start.3
  863.5 10.4 collective-permute-start.30
  873.9 2.5 collective-permute-start.31
  876.5 6.2 collective-permute-start.32
  882.7 4.0 collective-permute-start.33
  886.7 2.5 collective-permute-start.34
  889.2 3.2 collective-permute-start.35
  893.9 5.3 collective-permute-start.37
  899.2 2.1 fusion.151
  901.4 4.7 collective-permute-start.38
  907.4 9.4 collective-permute-start.4
  916.9 8.0 collective-permute-start.40
  924.9 3.8 collective-permute-start.41
  929.5 7.3 collective-permute-start.5
  936.8 13.1 %collective-permute-start.6 = (bf16[32,256]{1,0:T(8,128)(2,1)}, bf16[32,256]{1,0:T(8,128)(2,1)S(1)}, u32[]{:S(2)}, u32[]{:S(2)}) collective-permute-start(bf16[32,256]{1,0:T(8,128)(2,1)} %convert.79), channel_id=1, source_target_pairs={{0,4},{1,5},{2,6},{3,7},{4,8},{5,9},{6,10},{7,11},{8,12},{9,13},{1... | collective-permute-start | bytes 49160
  949.9 13.1 %collective-permute-start.7 = (bf16[32,256]{1,0:T(8,128)(2,1)}, bf16[32,256]{1,0:T(8,128)(2,1)S(1)}, u32[]{:S(2)}, u32[]{:S(2)}) collective-permute-start(bf16[32,256]{1,0:T(8,128)(2,1)} %convert.79), channel_id=1, source_target_pairs={{0,5},{1,6},{2,7},{3,8},{4,9},{5,10},{6,11},{7,12},{8,13},{9,14},{... | collective-permute-start | bytes 49160
  963.1 13.1 %collective-permute-start.8 = (bf16[32,256]{1,0:T(8,128)(2,1)}, bf16[32,256]{1,0:T(8,128)(2,1)S(1)}, u32[]{:S(2)}, u32[]{:S(2)}) collective-permute-start(bf16[32,256]{1,0:T(8,128)(2,1)} %convert.79), channel_id=1, source_target_pairs={{0,6},{1,7},{2,8},{3,9},{4,10},{5,11},{6,12},{7,13},{8,14},{9,15},... | collective-permute-start | bytes 49160
  976.2 13.3 %collective-permute-start.9 = (bf16[32,256]{1,0:T(8,128)(2,1)}, bf16[32,256]{1,0:T(8,128)(2,1)}, u32[]{:S(2)}, u32[]{:S(2)}) collective-permute-start(bf16[32,256]{1,0:T(8,128)(2,1)} %convert.79), channel_id=1, source_target_pairs={{0,7},{1,8},{2,9},{3,10},{4,11},{5,12},{6,13},{7,14},{8,15},{9,16}... | collective-permute-start | bytes 49160
  991.7 3.4 collective-permute-done.9
  995.1 56.9 %concatenate.8 = bf16[1307,256]{1,0:T(8,128)(2,1)} concatenate(bf16[27,256]{1,0:T(8,128)(2,1)} %copy-done.26, bf16[32,256]{1,0:T(8,128)(2,1)} %copy-done.48, bf16[32,256]{1,0:T(8,128)(2,1)} %copy-done.47, bf16[32,256]{1,0:T(8,128)(2,1)S(1)} %collective-permute-done.39, bf16[32,256]{1,0:T(8,128)(2,1)S(1)} %collective-permute-done.38, bf16[32,256]{1,0:T(8,128)(2,1)} %copy-done.46, ...), dimensions={0} | concatenate | bytes 1354752
  1066.2 60.2 %all-reduce.3 = (f32[32]{0:T(128)S(1)}, f32[32]{0:T(128)S(1)}) all-reduce(f32[32]{0:T(128)S(1)} %reduce_sum.37, f32[32]{0:T(128)S(1)} %reduce_sum.25), channel_id=1, replica_groups=mesh['tm'=8,'height'=4,'dp'=8] {'tm','height'}, use_global_device_ids=true, to_apply=%region_5.6 | all-reduce | flops 64 | bytes 512 | tf_op jit(solution)/shard_map/psum | solution.py:101
  (254 shorter events, 43.6 us)
Async XLA Ops:
  7.2 1046.2 %all-gather.2.cloned.1.call-start = ((), (), s32[]{:S(2)}) async-start(), calls=%async_computation | async-start | bytes 3981312 | tf_op jit(solution)/shard_map/all_gather | solution.py:90
  8.9 8.6 collective-permute-start
  17.6 11.8 %collective-permute-start.1 = (bf16[4,1,256,256]{3,2,0,1:T(8,128)(2,1)S(1)}, bf16[4,1,256,256]{3,2,0,1:T(8,128)(2,1)S(1)}, u32[]{:S(2)}, u32[]{:S(2)}) collective-permute-start(bf16[4,1,256,256]{3,2,0,1:T(8,128)(2,1)S(1)} %pad_maximum_fusion), channel_id=1, source_target_pairs={{0,8},{8,16},{16,24},{1,9},{9,17},{17,25},{2,10},{10,18},{18,26},{... | collective-permute-start | bytes 1572872 | tf_op jit(solution)/shard_map/ppermute | solution.py:21
  20.8 12.7 %collective-permute-start.2 = (bf16[4,1,256,256]{3,2,0,1:T(8,128)(2,1)S(1)}, bf16[4,1,256,256]{3,2,0,1:T(8,128)(2,1)S(1)}, u32[]{:S(2)}, u32[]{:S(2)}) collective-permute-start(bf16[4,1,256,256]{3,2,0,1:T(8,128)(2,1)S(1)} %pad_maximum_fusion), channel_id=1, source_target_pairs={{8,0},{16,8},{24,16},{9,1},{17,9},{25,17},{10,2},{18,10},{26,18},{... | collective-permute-start | bytes 1572872 | tf_op jit(solution)/shard_map/ppermute | solution.py:23
  699.0 94.0 %collective-permute-start.10 = (bf16[32,256]{1,0:T(8,128)(2,1)}, bf16[32,256]{1,0:T(8,128)(2,1)S(1)}, u32[]{:S(2)}, u32[]{:S(2)}) collective-permute-start(bf16[32,256]{1,0:T(8,128)(2,1)} %convert.79), channel_id=1, source_target_pairs={{0,8},{1,9},{2,10},{3,11},{4,12},{5,13},{6,14},{7,15},{8,16},{9,17... | collective-permute-start | bytes 49160
  767.4 33.1 %collective-permute-start.11 = (bf16[32,256]{1,0:T(8,128)(2,1)}, bf16[32,256]{1,0:T(8,128)(2,1)S(1)}, u32[]{:S(2)}, u32[]{:S(2)}) collective-permute-start(bf16[32,256]{1,0:T(8,128)(2,1)} %convert.79), channel_id=1, source_target_pairs={{0,9},{1,10},{2,11},{3,12},{4,13},{5,14},{6,15},{7,16},{8,17},{9,1... | collective-permute-start | bytes 49160
  771.8 36.9 %collective-permute-start.12 = (bf16[32,256]{1,0:T(8,128)(2,1)}, bf16[32,256]{1,0:T(8,128)(2,1)S(1)}, u32[]{:S(2)}, u32[]{:S(2)}) collective-permute-start(bf16[32,256]{1,0:T(8,128)(2,1)} %convert.79), channel_id=1, source_target_pairs={{0,10},{1,11},{2,12},{3,13},{4,14},{5,15},{6,16},{7,17},{8,18},{9,... | collective-permute-start | bytes 49160
  777.3 33.5 %collective-permute-start.13 = (bf16[32,256]{1,0:T(8,128)(2,1)}, bf16[32,256]{1,0:T(8,128)(2,1)S(1)}, u32[]{:S(2)}, u32[]{:S(2)}) collective-permute-start(bf16[32,256]{1,0:T(8,128)(2,1)} %convert.79), channel_id=1, source_target_pairs={{0,11},{1,12},{2,13},{3,14},{4,15},{5,16},{6,17},{7,18},{8,19},{9,... | collective-permute-start | bytes 49160
  783.1 4.6 collective-permute-start.42
  787.7 28.7 %collective-permute-start.14 = (bf16[32,256]{1,0:T(8,128)(2,1)}, bf16[32,256]{1,0:T(8,128)(2,1)S(1)}, u32[]{:S(2)}, u32[]{:S(2)}) collective-permute-start(bf16[32,256]{1,0:T(8,128)(2,1)} %convert.79), channel_id=1, source_target_pairs={{0,12},{1,13},{2,14},{3,15},{4,16},{5,17},{6,18},{7,19},{8,20},{9,... | collective-permute-start | bytes 49160
  792.9 26.0 %collective-permute-start.15 = (bf16[32,256]{1,0:T(8,128)(2,1)}, bf16[32,256]{1,0:T(8,128)(2,1)S(1)}, u32[]{:S(2)}, u32[]{:S(2)}) collective-permute-start(bf16[32,256]{1,0:T(8,128)(2,1)} %convert.79), channel_id=1, source_target_pairs={{0,13},{1,14},{2,15},{3,16},{4,17},{5,18},{6,19},{7,20},{8,21},{9,... | collective-permute-start | bytes 49160
  800.5 21.8 %collective-permute-start.16 = (bf16[32,256]{1,0:T(8,128)(2,1)}, bf16[32,256]{1,0:T(8,128)(2,1)S(1)}, u32[]{:S(2)}, u32[]{:S(2)}) collective-permute-start(bf16[32,256]{1,0:T(8,128)(2,1)} %convert.79), channel_id=1, source_target_pairs={{0,14},{1,15},{2,16},{3,17},{4,18},{5,19},{6,20},{7,21},{8,22},{9,... | collective-permute-start | bytes 49160
  808.6 19.5 %collective-permute-start.17 = (bf16[32,256]{1,0:T(8,128)(2,1)}, bf16[32,256]{1,0:T(8,128)(2,1)S(1)}, u32[]{:S(2)}, u32[]{:S(2)}) collective-permute-start(bf16[32,256]{1,0:T(8,128)(2,1)} %convert.79), channel_id=1, source_target_pairs={{0,15},{1,16},{2,17},{3,18},{4,19},{5,20},{6,21},{7,22},{8,23},{9,... | collective-permute-start | bytes 49160
  810.8 23.4 %collective-permute-start.18 = (bf16[32,256]{1,0:T(8,128)(2,1)}, bf16[32,256]{1,0:T(8,128)(2,1)S(1)}, u32[]{:S(2)}, u32[]{:S(2)}) collective-permute-start(bf16[32,256]{1,0:T(8,128)(2,1)} %convert.79), channel_id=1, source_target_pairs={{0,16},{1,17},{2,18},{3,19},{4,20},{5,21},{6,22},{7,23},{8,24},{9,... | collective-permute-start | bytes 49160
  816.4 24.8 %collective-permute-start.19 = (bf16[32,256]{1,0:T(8,128)(2,1)}, bf16[32,256]{1,0:T(8,128)(2,1)S(1)}, u32[]{:S(2)}, u32[]{:S(2)}) collective-permute-start(bf16[32,256]{1,0:T(8,128)(2,1)} %convert.79), channel_id=1, source_target_pairs={{0,17},{1,18},{2,19},{3,20},{4,21},{5,22},{6,23},{7,24},{8,25},{9,... | collective-permute-start | bytes 49160
  819.0 26.3 %collective-permute-start.20 = (bf16[32,256]{1,0:T(8,128)(2,1)}, bf16[32,256]{1,0:T(8,128)(2,1)S(1)}, u32[]{:S(2)}, u32[]{:S(2)}) collective-permute-start(bf16[32,256]{1,0:T(8,128)(2,1)} %convert.79), channel_id=1, source_target_pairs={{0,18},{1,19},{2,20},{3,21},{4,22},{5,23},{6,24},{7,25},{8,26},{9,... | collective-permute-start | bytes 49160
  822.2 25.0 %collective-permute-start.21 = (bf16[32,256]{1,0:T(8,128)(2,1)}, bf16[32,256]{1,0:T(8,128)(2,1)S(1)}, u32[]{:S(2)}, u32[]{:S(2)}) collective-permute-start(bf16[32,256]{1,0:T(8,128)(2,1)} %convert.79), channel_id=1, source_target_pairs={{0,19},{1,20},{2,21},{3,22},{4,23},{5,24},{6,25},{7,26},{8,27},{9,... | collective-permute-start | bytes 49160
  828.1 21.0 %collective-permute-start.22 = (bf16[32,256]{1,0:T(8,128)(2,1)}, bf16[32,256]{1,0:T(8,128)(2,1)S(1)}, u32[]{:S(2)}, u32[]{:S(2)}) collective-permute-start(bf16[32,256]{1,0:T(8,128)(2,1)} %convert.79), channel_id=1, source_target_pairs={{0,20},{1,21},{2,22},{3,23},{4,24},{5,25},{6,26},{7,27},{8,28},{9,... | collective-permute-start | bytes 49160
  834.2 17.1 %collective-permute-start.23 = (bf16[32,256]{1,0:T(8,128)(2,1)}, bf16[32,256]{1,0:T(8,128)(2,1)S(1)}, u32[]{:S(2)}, u32[]{:S(2)}) collective-permute-start(bf16[32,256]{1,0:T(8,128)(2,1)} %convert.79), channel_id=1, source_target_pairs={{0,21},{1,22},{2,23},{3,24},{4,25},{5,26},{6,27},{7,28},{8,29},{9,... | collective-permute-start | bytes 49160
  841.3 12.3 %collective-permute-start.24 = (bf16[32,256]{1,0:T(8,128)(2,1)}, bf16[32,256]{1,0:T(8,128)(2,1)S(1)}, u32[]{:S(2)}, u32[]{:S(2)}) collective-permute-start(bf16[32,256]{1,0:T(8,128)(2,1)} %convert.79), channel_id=1, source_target_pairs={{0,22},{1,23},{2,24},{3,25},{4,26},{5,27},{6,28},{7,29},{8,30},{9,... | collective-permute-start | bytes 49160
  845.3 10.8 collective-permute-start.25
  847.3 16.2 %collective-permute-start.26 = (bf16[32,256]{1,0:T(8,128)(2,1)}, bf16[32,256]{1,0:T(8,128)(2,1)S(1)}, u32[]{:S(2)}, u32[]{:S(2)}) collective-permute-start(bf16[32,256]{1,0:T(8,128)(2,1)} %convert.79), channel_id=1, source_target_pairs={{0,24},{1,25},{2,26},{3,27},{4,28},{5,29},{6,30},{7,31},{8,32},{9,... | collective-permute-start | bytes 49160
  849.2 24.7 %collective-permute-start.27 = (bf16[32,256]{1,0:T(8,128)(2,1)}, bf16[32,256]{1,0:T(8,128)(2,1)S(1)}, u32[]{:S(2)}, u32[]{:S(2)}) collective-permute-start(bf16[32,256]{1,0:T(8,128)(2,1)} %convert.79), channel_id=1, source_target_pairs={{0,25},{1,26},{2,27},{3,28},{4,29},{5,30},{6,31},{7,32},{8,33},{9,... | collective-permute-start | bytes 49160
  851.4 25.1 %collective-permute-start.28 = (bf16[32,256]{1,0:T(8,128)(2,1)}, bf16[32,256]{1,0:T(8,128)(2,1)S(1)}, u32[]{:S(2)}, u32[]{:S(2)}) collective-permute-start(bf16[32,256]{1,0:T(8,128)(2,1)} %convert.79), channel_id=1, source_target_pairs={{0,26},{1,27},{2,28},{3,29},{4,30},{5,31},{6,32},{7,33},{8,34},{9,... | collective-permute-start | bytes 49160
  853.6 29.1 %collective-permute-start.29 = (bf16[32,256]{1,0:T(8,128)(2,1)}, bf16[32,256]{1,0:T(8,128)(2,1)}, u32[]{:S(2)}, u32[]{:S(2)}) collective-permute-start(bf16[32,256]{1,0:T(8,128)(2,1)} %convert.79), channel_id=1, source_target_pairs={{0,27},{1,28},{2,29},{3,30},{4,31},{5,32},{6,33},{7,34},{8,35},{9,... | collective-permute-start | bytes 49160
  856.2 30.5 %collective-permute-start.3 = (bf16[32,256]{1,0:T(8,128)(2,1)}, bf16[32,256]{1,0:T(8,128)(2,1)}, u32[]{:S(2)}, u32[]{:S(2)}) collective-permute-start(bf16[32,256]{1,0:T(8,128)(2,1)} %convert.79), channel_id=1, source_target_pairs={{0,1},{1,2},{2,3},{3,4},{4,5},{5,6},{6,7},{7,8},{8,9},{9,10},{10,1... | collective-permute-start | bytes 49160
  863.5 25.8 %collective-permute-start.30 = (bf16[32,256]{1,0:T(8,128)(2,1)}, bf16[32,256]{1,0:T(8,128)(2,1)}, u32[]{:S(2)}, u32[]{:S(2)}) collective-permute-start(bf16[32,256]{1,0:T(8,128)(2,1)} %convert.79), channel_id=1, source_target_pairs={{0,28},{1,29},{2,30},{3,31},{4,32},{5,33},{6,34},{7,35},{8,36},{9,... | collective-permute-start | bytes 49160
  873.9 18.5 %collective-permute-start.31 = (bf16[32,256]{1,0:T(8,128)(2,1)}, bf16[32,256]{1,0:T(8,128)(2,1)}, u32[]{:S(2)}, u32[]{:S(2)}) collective-permute-start(bf16[32,256]{1,0:T(8,128)(2,1)} %convert.79), channel_id=1, source_target_pairs={{0,29},{1,30},{2,31},{3,32},{4,33},{5,34},{6,35},{7,36},{8,37},{9,... | collective-permute-start | bytes 49160
  876.5 17.2 %collective-permute-start.32 = (bf16[32,256]{1,0:T(8,128)(2,1)}, bf16[32,256]{1,0:T(8,128)(2,1)}, u32[]{:S(2)}, u32[]{:S(2)}) collective-permute-start(bf16[32,256]{1,0:T(8,128)(2,1)} %convert.79), channel_id=1, source_target_pairs={{0,30},{1,31},{2,32},{3,33},{4,34},{5,35},{6,36},{7,37},{8,38},{9,... | collective-permute-start | bytes 49160
  882.7 18.7 %collective-permute-start.33 = (bf16[32,256]{1,0:T(8,128)(2,1)}, bf16[32,256]{1,0:T(8,128)(2,1)S(1)}, u32[]{:S(2)}, u32[]{:S(2)}) collective-permute-start(bf16[32,256]{1,0:T(8,128)(2,1)} %convert.79), channel_id=1, source_target_pairs={{0,31},{1,32},{2,33},{3,34},{4,35},{5,36},{6,37},{7,38},{8,39},{9,... | collective-permute-start | bytes 49160
  886.7 19.4 %collective-permute-start.34 = (bf16[32,256]{1,0:T(8,128)(2,1)}, bf16[32,256]{1,0:T(8,128)(2,1)S(1)}, u32[]{:S(2)}, u32[]{:S(2)}) collective-permute-start(bf16[32,256]{1,0:T(8,128)(2,1)} %convert.79), channel_id=1, source_target_pairs={{0,32},{1,33},{2,34},{3,35},{4,36},{5,37},{6,38},{7,39},{8,40},{9,... | collective-permute-start | bytes 49160
  889.2 18.2 %collective-permute-start.35 = (bf16[32,256]{1,0:T(8,128)(2,1)}, bf16[32,256]{1,0:T(8,128)(2,1)S(1)}, u32[]{:S(2)}, u32[]{:S(2)}) collective-permute-start(bf16[32,256]{1,0:T(8,128)(2,1)} %convert.79), channel_id=1, source_target_pairs={{0,33},{1,34},{2,35},{3,36},{4,37},{5,38},{6,39},{7,40},{8,41},{9,... | collective-permute-start | bytes 49160
  892.4 24.4 %collective-permute-start.36 = (bf16[32,256]{1,0:T(8,128)(2,1)}, bf16[32,256]{1,0:T(8,128)(2,1)S(1)}, u32[]{:S(2)}, u32[]{:S(2)}) collective-permute-start(bf16[32,256]{1,0:T(8,128)(2,1)} %convert.79), channel_id=1, source_target_pairs={{0,34},{1,35},{2,36},{3,37},{4,38},{5,39},{6,40},{7,41},{8,42},{9,... | collective-permute-start | bytes 49160
  893.9 31.0 %collective-permute-start.37 = (bf16[32,256]{1,0:T(8,128)(2,1)}, bf16[32,256]{1,0:T(8,128)(2,1)S(1)}, u32[]{:S(2)}, u32[]{:S(2)}) collective-permute-start(bf16[32,256]{1,0:T(8,128)(2,1)} %convert.79), channel_id=1, source_target_pairs={{0,35},{1,36},{2,37},{3,38},{4,39},{5,40},{6,41},{7,42},{8,43},{9,... | collective-permute-start | bytes 49160
  901.3 152.0 %copy-start.16 = (bf16[2,1,256,256]{3,2,0,1:T(8,128)(2,1)S(1)}, bf16[2,1,256,256]{3,2,0,1:T(8,128)(2,1)}, u32[]{:S(2)}) copy-start(bf16[2,1,256,256]{3,2,0,1:T(8,128)(2,1)} %get-tuple-element.10) | copy-start | bytes 786436
  901.3 154.6 %copy-start.14 = (bf16[2,1,256,256]{3,2,0,1:T(8,128)(2,1)S(1)}, bf16[2,1,256,256]{3,2,0,1:T(8,128)(2,1)}, u32[]{:S(2)}) copy-start(bf16[2,1,256,256]{3,2,0,1:T(8,128)(2,1)} %get-tuple-element.12) | copy-start | bytes 786436
  901.4 155.8 %copy-start.13 = (bf16[2,1,256,256]{3,2,0,1:T(8,128)(2,1)S(1)}, bf16[2,1,256,256]{3,2,0,1:T(8,128)(2,1)}, u32[]{:S(2)}) copy-start(bf16[2,1,256,256]{3,2,0,1:T(8,128)(2,1)} %get-tuple-element.13) | copy-start | bytes 786436
  901.4 28.1 %collective-permute-start.38 = (bf16[32,256]{1,0:T(8,128)(2,1)}, bf16[32,256]{1,0:T(8,128)(2,1)S(1)}, u32[]{:S(2)}, u32[]{:S(2)}) collective-permute-start(bf16[32,256]{1,0:T(8,128)(2,1)} %convert.79), channel_id=1, source_target_pairs={{0,36},{1,37},{2,38},{3,39},{4,40},{5,41},{6,42},{7,43},{8,44},{9,... | collective-permute-start | bytes 49160
  906.1 30.7 %collective-permute-start.39 = (bf16[32,256]{1,0:T(8,128)(2,1)}, bf16[32,256]{1,0:T(8,128)(2,1)S(1)}, u32[]{:S(2)}, u32[]{:S(2)}) collective-permute-start(bf16[32,256]{1,0:T(8,128)(2,1)} %convert.79), channel_id=1, source_target_pairs={{0,37},{1,38},{2,39},{3,40},{4,41},{5,42},{6,43},{7,44},{8,45},{9,... | collective-permute-start | bytes 49160
  907.4 42.5 %collective-permute-start.4 = (bf16[32,256]{1,0:T(8,128)(2,1)}, bf16[32,256]{1,0:T(8,128)(2,1)S(1)}, u32[]{:S(2)}, u32[]{:S(2)}) collective-permute-start(bf16[32,256]{1,0:T(8,128)(2,1)} %convert.79), channel_id=1, source_target_pairs={{0,2},{1,3},{2,4},{3,5},{4,6},{5,7},{6,8},{7,9},{8,10},{9,11},{10,... | collective-permute-start | bytes 49160
  916.9 46.2 %collective-permute-start.40 = (bf16[32,256]{1,0:T(8,128)(2,1)}, bf16[32,256]{1,0:T(8,128)(2,1)S(1)}, u32[]{:S(2)}, u32[]{:S(2)}) collective-permute-start(bf16[32,256]{1,0:T(8,128)(2,1)} %convert.79), channel_id=1, source_target_pairs={{0,38},{1,39},{2,40},{3,41},{4,42},{5,43},{6,44},{7,45},{8,46},{9,... | collective-permute-start | bytes 49160
  924.9 51.3 %collective-permute-start.41 = (bf16[32,256]{1,0:T(8,128)(2,1)}, bf16[32,256]{1,0:T(8,128)(2,1)S(1)}, u32[]{:S(2)}, u32[]{:S(2)}) collective-permute-start(bf16[32,256]{1,0:T(8,128)(2,1)} %convert.79), channel_id=1, source_target_pairs={{0,39},{1,40},{2,41},{3,42},{4,43},{5,44},{6,45},{7,46},{8,47},{9,... | collective-permute-start | bytes 49160
  929.5 129.2 %copy-start.11 = (bf16[2,1,256,256]{3,2,0,1:T(8,128)(2,1)S(1)}, bf16[2,1,256,256]{3,2,0,1:T(8,128)(2,1)}, u32[]{:S(2)}) copy-start(bf16[2,1,256,256]{3,2,0,1:T(8,128)(2,1)} %get-tuple-element.16) | copy-start | bytes 786436
  929.5 61.0 %collective-permute-start.5 = (bf16[32,256]{1,0:T(8,128)(2,1)}, bf16[32,256]{1,0:T(8,128)(2,1)S(1)}, u32[]{:S(2)}, u32[]{:S(2)}) collective-permute-start(bf16[32,256]{1,0:T(8,128)(2,1)} %convert.79), channel_id=1, source_target_pairs={{0,3},{1,4},{2,5},{3,6},{4,7},{5,8},{6,9},{7,10},{8,11},{9,12},{10... | collective-permute-start | bytes 49160
  936.8 53.7 %collective-permute-start.6 = (bf16[32,256]{1,0:T(8,128)(2,1)}, bf16[32,256]{1,0:T(8,128)(2,1)S(1)}, u32[]{:S(2)}, u32[]{:S(2)}) collective-permute-start(bf16[32,256]{1,0:T(8,128)(2,1)} %convert.79), channel_id=1, source_target_pairs={{0,4},{1,5},{2,6},{3,7},{4,8},{5,9},{6,10},{7,11},{8,12},{9,13},{1... | collective-permute-start | bytes 49160
  949.9 40.6 %collective-permute-start.7 = (bf16[32,256]{1,0:T(8,128)(2,1)}, bf16[32,256]{1,0:T(8,128)(2,1)S(1)}, u32[]{:S(2)}, u32[]{:S(2)}) collective-permute-start(bf16[32,256]{1,0:T(8,128)(2,1)} %convert.79), channel_id=1, source_target_pairs={{0,5},{1,6},{2,7},{3,8},{4,9},{5,10},{6,11},{7,12},{8,13},{9,14},{... | collective-permute-start | bytes 49160
  963.1 27.5 %collective-permute-start.8 = (bf16[32,256]{1,0:T(8,128)(2,1)}, bf16[32,256]{1,0:T(8,128)(2,1)S(1)}, u32[]{:S(2)}, u32[]{:S(2)}) collective-permute-start(bf16[32,256]{1,0:T(8,128)(2,1)} %convert.79), channel_id=1, source_target_pairs={{0,6},{1,7},{2,8},{3,9},{4,10},{5,11},{6,12},{7,13},{8,14},{9,15},... | collective-permute-start | bytes 49160
  976.2 18.9 %collective-permute-start.9 = (bf16[32,256]{1,0:T(8,128)(2,1)}, bf16[32,256]{1,0:T(8,128)(2,1)}, u32[]{:S(2)}, u32[]{:S(2)}) collective-permute-start(bf16[32,256]{1,0:T(8,128)(2,1)} %convert.79), channel_id=1, source_target_pairs={{0,7},{1,8},{2,9},{3,10},{4,11},{5,12},{6,13},{7,14},{8,15},{9,16}... | collective-permute-start | bytes 49160
  (59 other events, 1874.8 us)
Sparse Core Ops, SparseCore 0:
  22.2 51.8 all-gather.1
where the time goes:
time: 1140 us; the launch traced here: 1130 us
  blocking collectives  696 us (61%)
  starting transfers between devices  295 us (26%)
  local copies, waits for them, and re-layouts  82 us (7%)
  matrix products  22.9 us (2%)
  between operations  16.6 us (1%)
  waiting for transfers between devices  16.3 us (1%)
    unnamed x1, blocking collectives  636 us
    unnamed x40, starting transfers between devices  286 us
    psum x1, blocking collectives, per_device(): lax.psum((local_first, local_second), ('tm', 'height'))  60.2 us
    unnamed x128, local copies, waits for them, and re-layouts  58.4 us
  transfers between devices with their start and end apart: 44, of which 5 were waited for; matrix products, arithmetic and copies ran while one was open for 64% of the time, Pallas kernels for 0%

commit v1 on v0

v1 whole, which is shorter than its diff:
```python
import functools

import jax
import jax.numpy as jnp
from jax import lax
from jax.experimental import pallas as pl
from jax.experimental.pallas import tpu as pltpu
from jax.sharding import PartitionSpec as P

CORES = 2
PER = 2
MESH = pl.DeviceIdType.MESH
F32 = jnp.float32
BF16 = jnp.bfloat16


def nt(a, b):
    return lax.dot_general(a, b, (((1,), (1,)), ((), ())), preferred_element_type=F32)


def nn(a, b):
    return lax.dot_general(a, b, (((1,), (0,)), ((), ())), preferred_element_type=F32)


def tn(a, b):
    return lax.dot_general(a, b, (((0,), (0,)), ((), ())), preferred_element_type=F32)


def fused(
    X, Y, Z,
    clip_frames, acts, cot, weight, centre, spread, gain, bias,
    out, wout,
    act_in, act_send, act_all, cots, w_all, w_rows, w_taps, lhs, grad, normed, slope,
    total, x_send, x_recv, row_sum, z_send, z_recv, s_send, s_recv, g_send, g_recv,
    act_sem, cot_sem, own_send, fwd_send, sis_send, halo_send, a_snd, a_rcv, w_snd, w_rcv,
    x_snd, x_rcv, z_snd, z_rcv, s_snd, s_rcv, g_snd, g_rcv,
):
    tm = lax.axis_index("tm")
    y = lax.axis_index("height")
    z = lax.axis_index("dp")
    x = tm // CORES
    c = tm % CORES
    span = CORES * PER
    cols, ch = cots.shape[2], cots.shape[3]
    chunk = act_all.shape[2]
    lead = 2
    halves = ch // 128

    def dev(xx, cc, yy, zz):
        return (xx * CORES + cc, yy, zz)

    def remote(src, dst, snd, rcv, target):
        return pltpu.make_async_remote_copy(
            src_ref=src, dst_ref=dst, send_sem=snd, recv_sem=rcv,
            device_id=target, device_id_type=MESH,
        )

    up, down = (y + 1) % Y, (y + Y - 1) % Y
    prev_x, next_x = (x + X - 1) % X, (x + 1) % X
    sister = dev(x, 1 - c, y, z)

    act_copy = pltpu.make_async_copy(acts, act_in, act_sem)
    act_copy.start()
    for k in range(PER):
        pltpu.make_async_copy(cot.at[k], cots.at[PER * c + k, y], cot_sem.at[PER * c + k, y]).start()

    barrier = pltpu.get_barrier_semaphore()
    partners = [
        dev(x, (c + dc) % CORES, (y + dy) % Y, z)
        for dc in range(CORES) for dy in range(Y) if dc or dy
    ]
    partners += [dev((x + dx) % X, c, y, z) for dx in range(1, X)]
    partners += [dev(x, c, y, (z + dz) % Z) for dz in range(1, Z)]
    for target in partners:
        pl.semaphore_signal(barrier, inc=1, device_id=target, device_id_type=MESH)

    @pl.when(c == 0)
    def _():
        pl.semaphore_signal(barrier, inc=1, device_id=dev(prev_x, 1, y, z), device_id_type=MESH)

    @pl.when(c == 1)
    def _():
        pl.semaphore_signal(barrier, inc=1, device_id=dev(next_x, 0, y, z), device_id_type=MESH)

    pl.semaphore_wait(barrier, len(partners) + 1)

    def cot_to(k, row, target, snd):
        src = cot.at[k] if row is None else cots.at[PER * c + k, row]
        at = y if row is None else row
        return remote(src, cots.at[PER * c + k, at], snd, cot_sem.at[PER * c + k, at], target)

    def halo_to(k, row, slot):
        src = cot.at[k] if row is None else cots.at[PER * c + k, row]
        at = y if row is None else row
        return remote(
            src, cots.at[span + k, at], halo_send.at[k, slot], cot_sem.at[span + k, at],
            dev(prev_x, k, y, z),
        )

    sends = []

    def go(copy):
        copy.start()
        sends.append(copy)

    for k in range(PER):
        ends = (up, down) if k == 0 else (down, up)
        for n, row in enumerate(ends):
            go(cot_to(k, None, dev(x, c, row, z), own_send.at[k, n]))
    for k in range(PER):
        go(cot_to(k, None, sister, sis_send.at[k, 0]))

        @pl.when(c == 0)
        def _():
            halo_to(k, None, 0).start()

    mine = (z % CORES) == c
    wsrc = weight.at[pl.ds(y * Z, Z)]

    @pl.when(mine)
    def _():
        pltpu.make_async_copy(wsrc, w_all.at[z // CORES], w_rcv.at[z // CORES]).start()
        for d in range(1, Z):
            remote(
                wsrc, w_all.at[z // CORES], w_snd.at[d - 1], w_rcv.at[z // CORES],
                dev(x, c, y, (z + d) % Z),
            ).start()

    row_id = lax.broadcasted_iota(jnp.int32, (ch, ch), 0)
    col_id = lax.broadcasted_iota(jnp.int32, (ch, ch), 1)
    half = ch // X
    per_core = half // CORES
    order = (
        ((row_id // Z) % X) * half + (row_id // (chunk * Y)) * per_core
        + ((row_id // chunk) % Y) * Z + row_id % Z
    )
    pick = jnp.where(order == col_id, 1.0, 0.0).astype(BF16)
    act_copy.wait()
    for k in range(PER):
        act_send[:, k] = nt(pick, act_in[k]).astype(BF16).reshape(CORES * Y, chunk, cols)
    around = [(dc, dy) for dc in range(CORES) for dy in range(Y) if dc or dy]
    for n, (dc, dy) in enumerate(around):
        cc, yy = (c + dc) % CORES, (y + dy) % Y
        go(remote(
            act_send.at[cc * Y + yy], act_all.at[pl.ds(PER * c, PER), y], a_snd.at[n], a_rcv.at[n],
            dev(x, cc, yy, z),
        ))
    act_all[pl.ds(PER * c, PER), y] = act_send[c * Y + y]

    def clear(s, _):
        grad[s] = jnp.zeros(grad.shape[1:], F32)
        for edge in (0, Y + 1):
            lhs[s, edge] = jnp.zeros(lhs.shape[2:], BF16)
        return 0

    lax.fori_loop(0, span, clear, 0)
    total[...] = jnp.zeros(total.shape, F32)

    def arrived(f, row):
        remote(
            cots.at[f, row], cots.at[f, row], own_send.at[0, 0], cot_sem.at[f, row], sister
        ).wait_recv()

    across = (y + 2) % Y
    steps = [(0, down, up), (1, up, down), (0, up, None), (1, down, None), (0, across, None), (1, across, None)]
    arrived_own = []
    seen = [1, 1]
    for k, row, on in steps:
        arrived(PER * c + k, row)
        if on is not None:
            go(cot_to(k, row, dev(x, c, on, z), fwd_send.at[k]))
        n = seen[k]
        seen[k] += 1
        go(cot_to(k, row, sister, sis_send.at[k, n]))

        @pl.when(c == 0)
        def _():
            halo_to(k, row, n).start()

    for k in range(PER):
        pltpu.make_async_copy(cot.at[k], cots.at[PER * c + k, y], cot_sem.at[PER * c + k, y]).wait()

    for n, (dc, dy) in enumerate(around):
        cs, ys = (c + dc) % CORES, (y + Y - dy) % Y
        remote(
            act_send.at[0], act_all.at[pl.ds(PER * cs, PER), ys], a_snd.at[n], a_rcv.at[n], sister
        ).wait_recv()

    i = lax.broadcasted_iota(jnp.int32, (chunk, 1), 0)
    channel = (i // Z) * half + c * per_core + y * Z + i % Z
    groups = centre.shape[1]
    group = (i // Z) * (groups // X) + c * (groups // X // CORES) + y

    def column(row, index):
        lane = lax.broadcasted_iota(jnp.int32, (chunk, row.shape[1]), 1)
        return jnp.sum(jnp.where(lane == index, row, 0.0), axis=1, keepdims=True)

    mean, scale = column(centre[...], group), column(spread[...], group)
    gains, biases = column(gain[...], channel), column(bias[...], channel)
    clip_len = clip_frames[0]

    def valid(f):
        return jnp.where(x * span + f < clip_len, 1.0, 0.0).astype(F32)

    lane = lax.broadcasted_iota(jnp.int32, (chunk, cols), 1)

    def prepare(t, _):
        s, r = t // Y, t % Y
        v = valid(s)
        norm = (act_all[s, r].astype(F32) - mean) * scale
        shifted = norm * gains + biases
        sig = jax.nn.sigmoid(shifted)
        normed[s, r] = norm
        slope[s, r] = sig * (1.0 + shifted * (1.0 - sig)) * v * gains
        a = shifted * sig * v
        lhs[s, r + 1, pl.ds(0, chunk)] = jnp.where(lane == 0, 0.0, pltpu.roll(a, 1, 1)).astype(BF16)
        lhs[s, r + 1, pl.ds(chunk, chunk)] = a.astype(BF16)
        lhs[s, r + 1, pl.ds(2 * chunk, chunk)] = jnp.where(
            lane == cols - 1, 0.0, pltpu.roll(a, cols - 1, 1)
        ).astype(BF16)
        return 0

    lax.fori_loop(0, span * Y, prepare, 0)

    rows3 = lhs.shape[2]

    def taps_of(f):
        return max(0, lead - f), min(3, span + lead - f)

    def masked(f, r):
        return jnp.where(x * span + f < clip_len, cots[f, r], jnp.zeros((cols, ch), BF16))

    def weight_term(f):
        k0, k1 = taps_of(f)
        s0, n = f - lead + k0, k1 - k0

        def body(r, _):
            left = lhs[pl.ds(s0, n), pl.ds(r, 3)].reshape(n * 3 * rows3, cols)
            total[pl.ds(k0, n)] += nn(left, masked(f, r)).reshape(n, 9, chunk, ch)
            return 0

        lax.fori_loop(0, Y, body, 0)

    tap_rows = 9 * Z

    def reduce_x(kt):
        for xx in range(X):
            x_send[kt, xx, pl.ds(0, tap_rows)] = (
                total[kt, :, pl.ds(xx * Z, Z)].reshape(tap_rows, ch).astype(BF16)
            )
            x_send[kt, xx, pl.ds(tap_rows, x_send.shape[2] - tap_rows)] = jnp.zeros(
                (x_send.shape[2] - tap_rows, ch), BF16
            )
        for d in range(1, X):
            xx = (x + d) % X
            go(remote(
                x_send.at[kt, xx], x_recv.at[kt, d - 1], x_snd.at[kt, d - 1], x_rcv.at[kt, d - 1],
                dev(xx, c, y, z),
            ))

    for f in range(span):
        @pl.when(c != f // PER)
        def _():
            for r in range(Y):
                arrived(f, r)

        weight_term(f)
    reduce_x(2)

    def halo_on(r, n):
        return remote(
            cots.at[span + c, r], cots.at[span + c, r], sis_send.at[n, Y], cot_sem.at[span + c, r], sister
        )

    for d in range(Y):
        r = (y + d) % Y
        arrived(span + c, r)
        copy = remote(
            cots.at[span + c, r], cots.at[span + c, r], fwd_send.at[PER + d], cot_sem.at[span + c, r], sister
        )
        go(copy)
    for f in range(span, span + lead):
        @pl.when(c != f - span)
        def _():
            for r in range(Y):
                arrived(f, r)

        weight_term(f)
        reduce_x(span + 1 - f)

    for n in range(X):
        pltpu.make_async_copy(w_all.at[n], w_all.at[n], w_rcv.at[n]).wait()

    def by_tap(i, _):
        rows = w_all[i // Z, i % Z].astype(F32)
        for h in range(halves):
            w_rows[h, pl.ds(i, 27, chunk), :] = rows[:, h * 128 : (h + 1) * 128]
        return 0

    lax.fori_loop(0, chunk, by_tap, 0)
    for h in range(halves):
        w_taps[:, :, :, pl.ds(h * 128, 128)] = w_rows[h].astype(BF16).reshape(w_taps.shape[:3] + (128,))

    def input_term(f):
        k0, k1 = taps_of(f)
        s0, n = f - lead + k0, k1 - k0

        def body(r, _):
            left = w_taps[pl.ds(k0, n)].reshape(n * 3 * rows3, ch)
            part = nt(left, masked(f, r)).reshape(n, 3, rows3, cols)
            grad[pl.ds(s0, n), pl.ds(r, 3)] += part
            return 0

        lax.fori_loop(0, Y, body, 0)

    for f in range(span + lead):
        input_term(f)

    def gather(t, carry):
        first, second = carry
        s, r = t // Y, t % Y
        g0 = grad[s, r + 1, pl.ds(0, chunk)]
        g1 = grad[s, r + 1, pl.ds(chunk, chunk)]
        g2 = grad[s, r + 1, pl.ds(2 * chunk, chunk)]
        whole = (
            jnp.where(lane == cols - 1, 0.0, pltpu.roll(g0, cols - 1, 1)) + g1
            + jnp.where(lane == 0, 0.0, pltpu.roll(g2, 1, 1))
        )
        upstream = whole * slope[s, r]
        slope[s, r] = upstream
        return first + upstream, second + upstream * normed[s, r]

    nothing = jnp.zeros((chunk, cols), F32)
    first, second = lax.fori_loop(0, span * Y, gather, (nothing, nothing))
    slim = lax.broadcasted_iota(jnp.int32, (chunk, 128), 1)
    first = jnp.sum(first, axis=1, keepdims=True)
    second = jnp.sum(second, axis=1, keepdims=True)
    s_send[...] = jnp.where(slim == 0, first, jnp.where(slim == 1, second, 0.0))
    for d in range(1, X):
        go(remote(
            s_send, s_recv.at[d - 1], s_snd.at[d - 1], s_rcv.at[d - 1], dev((x + d) % X, c, y, z)
        ))

    for kt in (2, 1, 0):
        for d in range(1, X):
            pltpu.make_async_copy(x_recv.at[kt, d - 1], x_recv.at[kt, d - 1], x_rcv.at[kt, d - 1]).wait()
        part = total[kt, :, pl.ds(x * Z, Z)].reshape(tap_rows, ch)
        for d in range(1, X):
            part = part + x_recv[kt, d - 1, pl.ds(0, tap_rows)].astype(F32)
        for h in range(halves):
            row_sum[h, pl.ds(kt * tap_rows, tap_rows)] = part[:, h * 128 : (h + 1) * 128]
    for zz in range(Z):
        for h in range(halves):
            z_send[zz, :, pl.ds(h * 128, 128)] = row_sum[h, pl.ds(zz, 27, Z), :]
    for d in range(1, Z):
        zz = (z + d) % Z
        go(remote(z_send.at[zz], z_recv.at[d - 1], z_snd.at[d - 1], z_rcv.at[d - 1], dev(x, c, y, zz)))

    for d in range(1, X):
        pltpu.make_async_copy(s_recv.at[d - 1], s_recv.at[d - 1], s_rcv.at[d - 1]).wait()
    both = s_send[...]
    for d in range(1, X):
        both = both + s_recv[d - 1]
    both = both.reshape(X, Z, 128)
    both = jnp.broadcast_to(jnp.sum(both, axis=1, keepdims=True), (X, Z, 128)).reshape(chunk, 128)
    population = clip_len.astype(F32) * (Y * cols * Z)
    first = jnp.sum(jnp.where(slim == 0, both, 0.0), axis=1, keepdims=True) / population
    second = jnp.sum(jnp.where(slim == 1, both, 0.0), axis=1, keepdims=True) / population

    def finish(t, _):
        s, r = t // Y, t % Y
        value = scale * (slope[s, r] - first - normed[s, r] * second) * valid(s)
        g_send[s, r] = value.astype(BF16)
        return 0

    lax.fori_loop(0, span * Y, finish, 0)
    for n, (dc, dy) in enumerate(around):
        cc, yy = (c + dc) % CORES, (y + dy) % Y
        go(remote(
            g_send.at[pl.ds(PER * cc, PER), yy], g_recv.at[c * Y + y], g_snd.at[n], g_rcv.at[n],
            dev(x, cc, yy, z),
        ))
    g_recv[c * Y + y] = g_send[pl.ds(PER * c, PER), y]

    for d in range(1, Z):
        pltpu.make_async_copy(z_recv.at[d - 1], z_recv.at[d - 1], z_rcv.at[d - 1]).wait()
    final = z_send[z]
    for d in range(1, Z):
        final = final + z_recv[d - 1]
    cells = X * Y * Z * CORES * PER * cols
    wout[...] = (final * (1.0 / cells)).astype(BF16)

    for n, (dc, dy) in enumerate(around):
        cs, ys = (c + dc) % CORES, (y + Y - dy) % Y
        remote(
            g_send.at[pl.ds(0, PER), 0], g_recv.at[cs * Y + ys], g_snd.at[n], g_rcv.at[n], sister
        ).wait_recv()
    for k in range(PER):
        out[k] = tn(g_recv[:, k].reshape(ch, cols), pick).astype(BF16)

    for copy in sends:
        copy.wait_send()

    @pl.when(c == 0)
    def _():
        for k in range(PER):
            for n in range(Y):
                halo_to(k, y, n).wait_send()

    @pl.when(mine)
    def _():
        for d in range(1, Z):
            remote(
                wsrc, w_all.at[z // CORES], w_snd.at[d - 1], w_rcv.at[z // CORES], sister
            ).wait_send()


def per_device(X, Y, Z, acts, cot, clip_frames, weight, centre, spread, gain, bias):
    _, per, _, cols, ch = acts.shape
    span, lead = CORES * per, 2
    chunk = ch // (CORES * Y)
    taps = weight.shape[1]
    dma = pltpu.SemaphoreType.DMA
    hbm = pl.BlockSpec(memory_space=pl.ANY)
    vmem = pl.BlockSpec(memory_space=pltpu.VMEM)
    tap_rows = -(-9 * Z // 16) * 16
    grad_input, weight_grad = pl.pallas_call(
        functools.partial(fused, X, Y, Z),
        out_shape=(
            jax.ShapeDtypeStruct((per, cols, ch), BF16),
            jax.ShapeDtypeStruct((taps, ch), BF16),
        ),
        in_specs=[pl.BlockSpec(memory_space=pltpu.SMEM), hbm, hbm, hbm, vmem, vmem, vmem, vmem],
        out_specs=(vmem, vmem),
        scratch_shapes=[
            pltpu.VMEM((per, cols, ch), BF16),
            pltpu.VMEM((CORES * Y, per, chunk, cols), BF16),
            pltpu.VMEM((span, Y, chunk, cols), BF16),
            pltpu.VMEM((span + lead, Y, cols, ch), BF16),
            pltpu.VMEM((X, Z, taps, ch), BF16),
            pltpu.VMEM((ch // 128, taps * chunk, 128), F32),
            pltpu.VMEM((3, 3, 3 * chunk, ch), BF16),
            pltpu.VMEM((span, Y + 2, 3 * chunk, cols), BF16),
            pltpu.VMEM((span, Y + 2, 3 * chunk, cols), F32),
            pltpu.VMEM((span, Y, chunk, cols), F32),
            pltpu.VMEM((span, Y, chunk, cols), F32),
            pltpu.VMEM((3, 9, chunk, ch), F32),
            pltpu.VMEM((3, X, tap_rows, ch), BF16),
            pltpu.VMEM((3, X - 1, tap_rows, ch), BF16),
            pltpu.VMEM((ch // 128, taps * Z, 128), F32),
            pltpu.VMEM((Z, taps, ch), F32),
            pltpu.VMEM((Z - 1, taps, ch), F32),
            pltpu.VMEM((chunk, 128), F32),
            pltpu.VMEM((X - 1, chunk, 128), F32),
            pltpu.VMEM((span, Y, chunk, cols), BF16),
            pltpu.VMEM((CORES * Y, per, chunk, cols), BF16),
            dma,
            dma((span + lead, Y)),
            dma((per, 2)),
            dma((per + Y,)),
            dma((per, Y)),
            dma((per, Y)),
            dma((CORES * Y - 1,)),
            dma((CORES * Y - 1,)),
            dma((Z - 1,)),
            dma((X,)),
            dma((3, X - 1)),
            dma((3, X - 1)),
            dma((Z - 1,)),
            dma((Z - 1,)),
            dma((X - 1,)),
            dma((X - 1,)),
            dma((CORES * Y - 1,)),
            dma((CORES * Y - 1,)),
        ],
        compiler_params=pltpu.CompilerParams(
            collective_id=0, has_side_effects=True, vmem_limit_bytes=48 * 1024 * 1024
        ),
    )(
        clip_frames,
        acts.reshape(per, cols, ch),
        cot.reshape(per, cols, ch),
        weight,
        centre,
        spread,
        gain.reshape(1, ch),
        bias.reshape(1, ch),
    )
    return grad_input.reshape(1, per, 1, cols, ch), weight_grad


def solution(mesh):
    X, Y, Z = mesh.shape["tm"] // CORES, mesh.shape["height"], mesh.shape["dp"]
    return jax.shard_map(
        functools.partial(per_device, X, Y, Z),
        mesh=mesh,
        in_specs=(
            P("dp", "tm", "height", None, None),
            P("dp", "tm", "height", None, None),
            P("dp"),
            P("dp", None, None),
            P("dp", None),
            P("dp", None),
            P(),
            P(),
        ),
        out_specs=(P("dp", "tm", "height", None, None), P(("tm", "height", "dp"), None)),
        check_vma=False,
    )
```

time: 1140 us -> 56.2 us (0.05)
  blocking collectives: 696 us -> 0 us
  starting transfers between devices: 295 us -> 0 us
  local copies, waits for them, and re-layouts: 82 us -> 2.64 us
  Pallas kernels: 0 us -> 52.1 us
  matrix products: 22.9 us -> 0 us
  waiting for transfers between devices: 16.3 us -> 0 us
  between operations: 16.6 us -> 1.38 us
    unnamed x1 -> x0, blocking collectives: 636 us -> none
    unnamed x40 -> x0, starting transfers between devices: 286 us -> none
    psum x1 -> x0, blocking collectives: 60.2 us -> none  [per_device(): lax.psum((local_first, local_second), ('tm', 'height'))]
    unnamed x128 -> x15, local copies, waits for them, and re-layouts: 58.4 us -> 2.64 us
    pallas_call x0 -> x1, Pallas kernels: none -> 52.1 us  [per_device(): pl.pallas_call(functools.partial(fused, X, Y, Z), out_shape=(jax.ShapeDty...]
    dot_general x54 -> x0, matrix products: 22.9 us -> none  [the longest x27 11.5 us: contract_inner(): lax.dot_general(matrix, operand, (((1,), (1,)), ((), ())), preferred_elem...]
    mul x7 -> x0, local copies, waits for them, and re-layouts: 17.3 us -> none  [the longest x2 16.2 us: per_device(): jnp.stack(per_tap, axis=1) * inv_cells]
    ppermute x3 -> x0, waiting for transfers between devices: 11.9 us -> none  [the longest x1 4.41 us: padded_2(): lax.ppermute(tail, axis, [(i, (i + 1) % count) for i in range(ends)])]
  transfers between devices with their start and end apart: 44 -> 0, of which waited for: 5 -> 0; matrix products, arithmetic and copies ran while one was open for 64% -> 0% of each run, Pallas kernels for 0% -> 0%
where the time goes in v1:
time: 56.2 us; the launch traced here: 56.1 us
  Pallas kernels  52.1 us (93%)
  local copies, waits for them, and re-layouts  2.64 us (5%)
  between operations  1.38 us (2%)
    pallas_call x1, Pallas kernels, per_device(): pl.pallas_call(functools.partial(fused, X, Y, Z), out_shape=(jax.ShapeDty...  52.1 us
    unnamed x15, local copies, waits for them, and re-layouts  2.64 us

profile of v1, /device:TPU:1, one launch (start us, length us, event | category | flops | bytes accessed | tf_op | source)
XLA Modules:
  0.0 56.1 jit_solution(10825671066707281775)
XLA Ops:
  1.3 0.0 copy-start
  1.3 0.0 copy-start.1
  1.3 0.0 copy-start.2
  1.3 0.0 copy-start.3
  1.3 0.0 copy-start.4
  1.3 0.0 copy-start.5
  1.3 1.3 %copy.10.weight = bf16[32,27,256]{2,1,0:T(8,128)(2,1)S(1)} copy(bf16[32,27,256]{2,0,1:T(8,128)(2,1)} %param.11) | data formatting | bytes 884736 | tf_op args[3]
  2.6 0.0 copy-done
  2.7 0.0 copy-done.1
  2.7 0.0 copy-done.2
  2.7 0.0 copy-done.3
  2.7 0.0 copy-done.4
  2.7 0.0 copy-done.5
  2.7 52.1 %shard_map.95 = (bf16[2,256,256]{2,1,0:T(8,128)(2,1)S(1)}, bf16[27,256]{1,0:T(8,128)(2,1)S(1)}) custom-call(s32[1]{0:T(128)S(6)} %copy.14.clip_frames, bf16[2,256,256]{2,1,0:T(8,128)(2,1)S(1)} %bitcast.7, bf16[2,256,256]{2,1,0:T(8,128)(2,1)S(1)} %bitcast.8, bf16[32,27,256]{2,1,0:T(8,128)(2,1)S(1)} %copy.10.weight, f32[1,32]{1,0:T(1,128)S(1)} %copy-done.4, ...), custom_call_target="tpu_custom_call" | custom-call | tf_op jit(solution)/shard_map/pallas_call | solution.py:427
  54.8 0.7 %copy.15 = bf16[1,2,1,256,256]{4,3,2,1,0:T(8,128)(2,1)} copy(bf16[1,2,1,256,256]{4,3,2,1,0:T(8,128)(2,1)S(1)} %bitcast.9) | data formatting | bytes 524288
  55.5 0.6 %copy.16 = bf16[27,256]{1,0:T(8,128)(2,1)} copy(bf16[27,256]{1,0:T(8,128)(2,1)S(1)} %get-tuple-element.11) | data formatting | bytes 27648
Async XLA Ops:
  1.3 1.4 %copy-start = (bf16[1,2,1,256,256]{4,3,2,1,0:T(8,128)(2,1)S(1)}, bf16[1,2,1,256,256]{4,3,2,1,0:T(8,128)(2,1)}, u32[]{:S(2)}) copy-start(bf16[1,2,1,256,256]{4,3,2,1,0:T(8,128)(2,1)} %param.8) | copy-start | bytes 786436
  1.3 1.4 %copy-start.1 = (bf16[1,2,1,256,256]{4,3,2,1,0:T(8,128)(2,1)S(1)}, bf16[1,2,1,256,256]{4,3,2,1,0:T(8,128)(2,1)}, u32[]{:S(2)}) copy-start(bf16[1,2,1,256,256]{4,3,2,1,0:T(8,128)(2,1)} %param.9) | copy-start | bytes 786436
  1.3 1.4 %copy-start.2 = (f32[256]{0:T(256)S(1)}, f32[256]{0:T(256)}, u32[]{:S(2)}) copy-start(f32[256]{0:T(256)} %param.14) | copy-start | bytes 3076
  1.3 1.4 %copy-start.3 = (f32[256]{0:T(256)S(1)}, f32[256]{0:T(256)}, u32[]{:S(2)}) copy-start(f32[256]{0:T(256)} %param.15) | copy-start | bytes 3076
  1.3 1.4 %copy-start.4 = (f32[1,32]{1,0:T(1,128)S(1)}, f32[1,32]{1,0:T(1,128)}, u32[]{:S(2)}) copy-start(f32[1,32]{1,0:T(1,128)} %centre.1) | copy-start | bytes 388
  1.3 1.4 %copy-start.5 = (f32[1,32]{1,0:T(1,128)S(1)}, f32[1,32]{1,0:T(1,128)}, u32[]{:S(2)}) copy-start(f32[1,32]{1,0:T(1,128)} %spread.1) | copy-start | bytes 388

commit v2 on v1

v2 whole, which is shorter than its diff:
```python
import functools

import jax
import jax.numpy as jnp
from jax import lax
from jax.experimental import pallas as pl
from jax.experimental.pallas import tpu as pltpu
from jax.sharding import PartitionSpec as P

CORES = 2
PER = 2
MESH = pl.DeviceIdType.MESH
F32 = jnp.float32
BF16 = jnp.bfloat16


def nt(a, b):
    return lax.dot_general(a, b, (((1,), (1,)), ((), ())), preferred_element_type=F32)


def nn(a, b):
    return lax.dot_general(a, b, (((1,), (0,)), ((), ())), preferred_element_type=F32)


def tn(a, b):
    return lax.dot_general(a, b, (((0,), (0,)), ((), ())), preferred_element_type=F32)


def fused(
    X, Y, Z,
    clip_frames, acts, cot, weight, centre, spread, gain, bias,
    out, wout,
    act_in, act_send, act_all, cots, w_all, w_taps, lhs, grad, normed, slope,
    total, x_send, x_recv, row_sum, z_send, z_recv, s_send, s_recv, g_send, g_recv,
    act_sem, cot_sem, own_send, fwd_send, sis_send, halo_send, a_snd, a_rcv, w_snd, w_rcv,
    x_snd, x_rcv, z_snd, z_rcv, s_snd, s_rcv, g_snd, g_rcv, p_snd, p_rcv, z_ready,
):
    tm = lax.axis_index("tm")
    y = lax.axis_index("height")
    z = lax.axis_index("dp")
    x = tm // CORES
    c = tm % CORES
    span = CORES * PER
    cols, ch = cots.shape[2], cots.shape[3]
    chunk = act_all.shape[2]
    lead = 2
    halves = ch // 128

    def dev(xx, cc, yy, zz):
        return (xx * CORES + cc, yy, zz)

    def remote(src, dst, snd, rcv, target):
        return pltpu.make_async_remote_copy(
            src_ref=src, dst_ref=dst, send_sem=snd, recv_sem=rcv,
            device_id=target, device_id_type=MESH,
        )

    up, down = (y + 1) % Y, (y + Y - 1) % Y
    prev_x, next_x = (x + X - 1) % X, (x + 1) % X
    sister = dev(x, 1 - c, y, z)

    act_copy = pltpu.make_async_copy(acts, act_in, act_sem)
    act_copy.start()
    for k in range(PER):
        pltpu.make_async_copy(cot.at[k], cots.at[PER * c + k, y], cot_sem.at[PER * c + k, y]).start()

    barrier = pltpu.get_barrier_semaphore()
    partners = [
        dev(x, (c + dc) % CORES, (y + dy) % Y, z)
        for dc in range(CORES) for dy in range(Y) if dc or dy
    ]
    partners += [dev((x + dx) % X, c, y, z) for dx in range(1, X)]
    for target in partners:
        pl.semaphore_signal(barrier, inc=1, device_id=target, device_id_type=MESH)

    @pl.when(c == 0)
    def _():
        pl.semaphore_signal(barrier, inc=1, device_id=dev(prev_x, 1, y, z), device_id_type=MESH)

    @pl.when(c == 1)
    def _():
        pl.semaphore_signal(barrier, inc=1, device_id=dev(next_x, 0, y, z), device_id_type=MESH)

    for d in range(1, Z):
        @pl.when(z + d < Z)
        def _():
            pl.semaphore_signal(
                barrier, inc=1, device_id=dev(x, c, y, (z + d) % Z), device_id_type=MESH
            )

    row_id = lax.broadcasted_iota(jnp.int32, (ch, ch), 0)
    col_id = lax.broadcasted_iota(jnp.int32, (ch, ch), 1)
    half = ch // X
    per_core = half // CORES
    order = (
        ((row_id // Z) % X) * half + (row_id // (chunk * Y)) * per_core
        + ((row_id // chunk) % Y) * Z + row_id % Z
    )
    pick = jnp.where(order == col_id, 1.0, 0.0).astype(BF16)
    act_copy.wait()
    for k in range(PER):
        act_send[:, k] = nt(pick, act_in[k]).astype(BF16).reshape(CORES * Y, chunk, cols)

    pl.semaphore_wait(barrier, len(partners) + 1 + z)

    def cot_to(k, row, target, snd):
        src = cot.at[k] if row is None else cots.at[PER * c + k, row]
        at = y if row is None else row
        return remote(src, cots.at[PER * c + k, at], snd, cot_sem.at[PER * c + k, at], target)

    def halo_to(k, row, slot):
        src = cot.at[k] if row is None else cots.at[PER * c + k, row]
        at = y if row is None else row
        return remote(
            src, cots.at[span + k, at], halo_send.at[k, slot], cot_sem.at[span + k, at],
            dev(prev_x, k, y, z),
        )

    sends = []

    def go(copy):
        copy.start()
        sends.append(copy)

    around = [(dc, dy) for dc in range(CORES) for dy in range(Y) if dc or dy]
    for n, (dc, dy) in enumerate(around):
        cc, yy = (c + dc) % CORES, (y + dy) % Y
        go(remote(
            act_send.at[cc * Y + yy], act_all.at[pl.ds(lead + PER * c, PER), y], a_snd.at[n], a_rcv.at[n],
            dev(x, cc, yy, z),
        ))
    act_all[pl.ds(lead + PER * c, PER), y] = act_send[c * Y + y]

    for k in range(PER):
        ends = (up, down) if k == 0 else (down, up)
        for n, row in enumerate(ends):
            go(cot_to(k, None, dev(x, c, row, z), own_send.at[k, n]))
    for k in range(PER):
        go(cot_to(k, None, sister, sis_send.at[k, 0]))

        @pl.when(c == 0)
        def _():
            halo_to(k, None, 0).start()

    for d in range(1, Z):
        @pl.when(z >= d)
        def _():
            pl.semaphore_signal(
                z_ready, inc=1, device_id=dev(x, c, y, (z + Z - d) % Z), device_id_type=MESH
            )

    mine = (z % CORES) == c
    wsrc = weight.at[:, y]

    def weight_to(d):
        return remote(
            wsrc, w_all.at[:, z // CORES], w_snd.at[d - 1], w_rcv.at[z // CORES],
            dev(x, c, y, (z + d) % Z),
        )

    @pl.when(mine)
    def _():
        pltpu.make_async_copy(wsrc, w_all.at[:, z // CORES], w_rcv.at[z // CORES]).start()
        for d in range(1, Z):
            @pl.when(z + d >= Z)
            def _():
                weight_to(d).start()

    def clear(s, _):
        grad[s] = jnp.zeros(grad.shape[1:], F32)
        return 0

    def clear_edges(s, _):
        for edge in (0, Y + 1):
            lhs[s, edge] = jnp.zeros(lhs.shape[2:], BF16)
        return 0

    lax.fori_loop(0, span, clear, 0)
    lax.fori_loop(0, span + lead, clear_edges, 0)
    total[...] = jnp.zeros(total.shape, F32)

    def arrived(f, row):
        remote(
            cots.at[f, row], cots.at[f, row], own_send.at[0, 0], cot_sem.at[f, row], sister
        ).wait_recv()

    for n, (dc, dy) in enumerate(around):
        cs, ys = (c + dc) % CORES, (y + Y - dy) % Y
        remote(
            act_send.at[0], act_all.at[pl.ds(lead + PER * cs, PER), ys], a_snd.at[n], a_rcv.at[n], sister
        ).wait_recv()

    go(remote(
        act_all.at[pl.ds(span, lead)], act_all.at[pl.ds(0, lead)], p_snd, p_rcv, dev(next_x, c, y, z)
    ))

    i = lax.broadcasted_iota(jnp.int32, (chunk, 1), 0)
    channel = (i // Z) * half + c * per_core + y * Z + i % Z
    groups = centre.shape[1]
    group = (i // Z) * (groups // X) + c * (groups // X // CORES) + y

    def column(row, index):
        lane = lax.broadcasted_iota(jnp.int32, (chunk, row.shape[1]), 1)
        return jnp.sum(jnp.where(lane == index, row, 0.0), axis=1, keepdims=True)

    mean, scale = column(centre[...], group), column(spread[...], group)
    gains, biases = column(gain[...], channel), column(bias[...], channel)
    clip_len = clip_frames[0]

    def valid(f):
        t = x * span + f
        return jnp.where((t >= 0) & (t < clip_len), 1.0, 0.0).astype(F32)

    lane = lax.broadcasted_iota(jnp.int32, (chunk, cols), 1)

    def block_input(s, r):
        norm = (act_all[s + lead, r].astype(F32) - mean) * scale
        shifted = norm * gains + biases
        sig = jax.nn.sigmoid(shifted)
        a = shifted * sig * valid(s)
        at = s + lead
        lhs[at, r + 1, pl.ds(0, chunk)] = jnp.where(lane == 0, 0.0, pltpu.roll(a, 1, 1)).astype(BF16)
        lhs[at, r + 1, pl.ds(chunk, chunk)] = a.astype(BF16)
        lhs[at, r + 1, pl.ds(2 * chunk, chunk)] = jnp.where(
            lane == cols - 1, 0.0, pltpu.roll(a, cols - 1, 1)
        ).astype(BF16)
        return norm, shifted, sig

    def prepare(t, _):
        s, r = t // Y, t % Y
        norm, shifted, sig = block_input(s, r)
        normed[s, r] = norm
        slope[s, r] = sig * (1.0 + shifted * (1.0 - sig)) * valid(s) * gains
        return 0

    def prepare_before(t, _):
        block_input(t // Y - lead, t % Y)
        return 0

    lax.fori_loop(0, span * Y, prepare, 0)

    rows3 = lhs.shape[2]

    def taps_of(f):
        return max(0, lead - f), min(3, span + lead - f)

    def masked(f, r):
        return jnp.where(x * span + f < clip_len, cots[f, r], jnp.zeros((cols, ch), BF16))

    def weight_row(r):
        def body(f, _):
            @pl.when(c != f // PER)
            def _():
                arrived(f, r)

            left = lhs[pl.ds(f, 3), pl.ds(r, 3)].reshape(9 * rows3, cols)
            total[pl.ds(0, 27)] += nn(left, masked(f, r)).reshape(27, chunk, ch)
            return 0

        lax.fori_loop(0, span, body, 0)

    parts = [(t, min(8, 27 - t)) for t in range(0, 27, 8)]

    def sent_rows(taps):
        return -(-taps * Z // 16) * 16

    def reduce_x(j):
        tap, taps = parts[j]
        rows, whole = taps * Z, sent_rows(taps)
        for xx in range(X):
            x_send[j, xx, pl.ds(0, rows)] = (
                total[pl.ds(tap, taps), pl.ds(xx * Z, Z)].reshape(rows, ch).astype(BF16)
            )
            if whole > rows:
                x_send[j, xx, pl.ds(rows, whole - rows)] = jnp.zeros((whole - rows, ch), BF16)
        for d in range(1, X):
            xx = (x + d) % X
            go(remote(
                x_send.at[j, xx, pl.ds(0, whole)], x_recv.at[j, d - 1, pl.ds(0, whole)],
                x_snd.at[j, d - 1], x_rcv.at[j, d - 1], dev(xx, c, y, z),
            ))

    def reduce_z(j):
        tap, taps = parts[j]
        rows, whole = taps * Z, sent_rows(taps)
        for d in range(1, X):
            got = x_recv.at[j, d - 1, pl.ds(0, whole)]
            pltpu.make_async_copy(got, got, x_rcv.at[j, d - 1]).wait()
        part = total[pl.ds(tap, taps), pl.ds(x * Z, Z)].reshape(rows, ch)
        for d in range(1, X):
            part = part + x_recv[j, d - 1, pl.ds(0, rows)].astype(F32)
        for h in range(halves):
            row_sum[h, pl.ds(0, rows)] = part[:, h * 128 : (h + 1) * 128]
        for zz in range(Z):
            for h in range(halves):
                z_send[j, zz, :, pl.ds(h * 128, 128)] = row_sum[h, pl.ds(zz, 8, Z), :]
        for d in range(1, Z):
            zz = (z + d) % Z
            go(remote(
                z_send.at[j, zz], z_recv.at[j, d - 1], z_snd.at[j, d - 1], z_rcv.at[j, d - 1],
                dev(x, c, y, zz),
            ))


    across = (y + 2) % Y
    seen = [1, 1]

    def take(k, row, on):
        arrived(PER * c + k, row)
        if on is not None:
            go(cot_to(k, row, dev(x, c, on, z), fwd_send.at[k]))
        n = seen[k]
        seen[k] += 1
        go(cot_to(k, row, sister, sis_send.at[k, n]))

        @pl.when(c == 0)
        def _():
            halo_to(k, row, n).start()

    take(0, down, up)
    take(0, up, None)

    @pl.when(z < Z - 1)
    def _():
        pl.semaphore_wait(z_ready, Z - 1 - z)

    @pl.when(mine)
    def _():
        for d in range(1, Z):
            @pl.when(z + d < Z)
            def _():
                weight_to(d).start()

    pltpu.make_async_copy(act_all.at[pl.ds(0, lead)], act_all.at[pl.ds(0, lead)], p_rcv).wait()
    lax.fori_loop(0, lead * Y, prepare_before, 0)
    take(1, up, down)
    take(1, down, None)
    for k in range(PER):
        arrived(PER * c + k, y)

    def turn(n):
        return (y + n + (n // 2) * (1 - 2 * (n % 2))) % Y

    def early(n, _):
        weight_row(turn(n))
        return 0

    lax.fori_loop(0, Y - 1, early, 0)

    def halo_on(d):
        r = (y + d) % Y
        arrived(span + c, r)
        go(remote(
            cots.at[span + c, r], cots.at[span + c, r], fwd_send.at[PER + d], cot_sem.at[span + c, r],
            sister,
        ))

    halo_on(0)
    take(0, across, None)
    take(1, across, None)
    weight_row(across)
    row_sum[...] = jnp.zeros(row_sum.shape, F32)
    for j in range(len(parts)):
        reduce_x(j)
    halo_on(1)
    halo_on(3)

    for n in range(X):
        pltpu.make_async_copy(w_all.at[:, n], w_all.at[:, n], w_rcv.at[n]).wait()

    def by_tap(k, _):
        tap = w_all[pl.ds(3 * k, 3)].astype(F32).reshape(rows3, ch)
        w_taps[k // 3, k % 3] = tap.astype(BF16)
        return 0

    lax.fori_loop(0, 9, by_tap, 0)

    def input_term(f, r):
        k0, k1 = taps_of(f)
        s0, n = f - lead + k0, k1 - k0
        left = w_taps[pl.ds(k0, n)].reshape(n * 3 * rows3, ch)
        grad[pl.ds(s0, n), pl.ds(r, 3)] += nt(left, masked(f, r)).reshape(n, 3, rows3, cols)

    def input_row(r):
        for f in range(span):
            input_term(f, r)

    for n in range(Y - 1):
        input_row(turn(n))
        reduce_z(n)
    reduce_z(3)
    halo_on(2)
    input_row(across)
    for f in range(span, span + lead):
        def halo_input(r, _):
            @pl.when(c != f - span)
            def _():
                arrived(f, r)

            input_term(f, r)
            return 0

        lax.fori_loop(0, Y, halo_input, 0)

    def gather(t, carry):
        first, second = carry
        s, r = t // Y, t % Y
        g0 = grad[s, r + 1, pl.ds(0, chunk)]
        g1 = grad[s, r + 1, pl.ds(chunk, chunk)]
        g2 = grad[s, r + 1, pl.ds(2 * chunk, chunk)]
        whole = (
            jnp.where(lane == cols - 1, 0.0, pltpu.roll(g0, cols - 1, 1)) + g1
            + jnp.where(lane == 0, 0.0, pltpu.roll(g2, 1, 1))
        )
        upstream = whole * slope[s, r]
        slope[s, r] = upstream
        return first + upstream, second + upstream * normed[s, r]

    nothing = jnp.zeros((chunk, cols), F32)
    first, second = lax.fori_loop(0, span * Y, gather, (nothing, nothing))
    slim = lax.broadcasted_iota(jnp.int32, (chunk, 128), 1)
    first = jnp.sum(first, axis=1, keepdims=True)
    second = jnp.sum(second, axis=1, keepdims=True)
    s_send[...] = jnp.where(slim == 0, first, jnp.where(slim == 1, second, 0.0))
    for d in range(1, X):
        go(remote(
            s_send, s_recv.at[d - 1], s_snd.at[d - 1], s_rcv.at[d - 1], dev((x + d) % X, c, y, z)
        ))

    for d in range(1, X):
        pltpu.make_async_copy(s_recv.at[d - 1], s_recv.at[d - 1], s_rcv.at[d - 1]).wait()
    both = s_send[...]
    for d in range(1, X):
        both = both + s_recv[d - 1]
    both = both.reshape(X, Z, 128)
    both = jnp.broadcast_to(jnp.sum(both, axis=1, keepdims=True), (X, Z, 128)).reshape(chunk, 128)
    population = clip_len.astype(F32) * (Y * cols * Z)
    first = jnp.sum(jnp.where(slim == 0, both, 0.0), axis=1, keepdims=True) / population
    second = jnp.sum(jnp.where(slim == 1, both, 0.0), axis=1, keepdims=True) / population

    def finish(t, _):
        s, r = t // Y, t % Y
        value = scale * (slope[s, r] - first - normed[s, r] * second) * valid(s)
        g_send[s, r] = value.astype(BF16)
        return 0

    lax.fori_loop(0, span * Y, finish, 0)
    for n, (dc, dy) in enumerate(around):
        cc, yy = (c + dc) % CORES, (y + dy) % Y
        go(remote(
            g_send.at[pl.ds(PER * cc, PER), yy], g_recv.at[c * Y + y], g_snd.at[n], g_rcv.at[n],
            dev(x, cc, yy, z),
        ))
    g_recv[c * Y + y] = g_send[pl.ds(PER * c, PER), y]

    final = z_send[:, z]
    for j in range(len(parts)):
        for d in range(1, Z):
            pltpu.make_async_copy(z_recv.at[j, d - 1], z_recv.at[j, d - 1], z_rcv.at[j, d - 1]).wait()
    for d in range(1, Z):
        final = final + z_recv[:, d - 1]
    final = final.reshape(len(parts) * 8, ch)[:27]
    cells = X * Y * Z * CORES * PER * cols
    wout[...] = (final * (1.0 / cells)).astype(BF16)

    for n, (dc, dy) in enumerate(around):
        cs, ys = (c + dc) % CORES, (y + Y - dy) % Y
        remote(
            g_send.at[pl.ds(0, PER), 0], g_recv.at[cs * Y + ys], g_snd.at[n], g_rcv.at[n], sister
        ).wait_recv()
    for k in range(PER):
        out[k] = tn(g_recv[:, k].reshape(ch, cols), pick).astype(BF16)

    for copy in sends:
        copy.wait_send()

    @pl.when(c == 0)
    def _():
        for k in range(PER):
            for n in range(Y):
                halo_to(k, y, n).wait_send()

    @pl.when(mine)
    def _():
        for d in range(1, Z):
            weight_to(d).wait_send()


def per_device(X, Y, Z, acts, cot, clip_frames, weight, centre, spread, gain, bias):
    _, per, _, cols, ch = acts.shape
    span, lead = CORES * per, 2
    chunk = ch // (CORES * Y)
    taps = weight.shape[1]
    dma = pltpu.SemaphoreType.DMA
    hbm = pl.BlockSpec(memory_space=pl.ANY)
    vmem = pl.BlockSpec(memory_space=pltpu.VMEM)
    grad_input, weight_grad = pl.pallas_call(
        functools.partial(fused, X, Y, Z),
        out_shape=(
            jax.ShapeDtypeStruct((per, cols, ch), BF16),
            jax.ShapeDtypeStruct((taps, ch), BF16),
        ),
        in_specs=[pl.BlockSpec(memory_space=pltpu.SMEM), hbm, hbm, hbm, vmem, vmem, vmem, vmem],
        out_specs=(vmem, vmem),
        scratch_shapes=[
            pltpu.VMEM((per, cols, ch), BF16),
            pltpu.VMEM((CORES * Y, per, chunk, cols), BF16),
            pltpu.VMEM((span + lead, Y, chunk, cols), BF16),
            pltpu.VMEM((span + lead, Y, cols, ch), BF16),
            pltpu.VMEM((taps, X, Z, ch), BF16),
            pltpu.VMEM((3, 3, 3 * chunk, ch), BF16),
            pltpu.VMEM((span + lead, Y + 2, 3 * chunk, cols), BF16),
            pltpu.VMEM((span, Y + 2, 3 * chunk, cols), F32),
            pltpu.VMEM((span, Y, chunk, cols), F32),
            pltpu.VMEM((span, Y, chunk, cols), F32),
            pltpu.VMEM((taps, chunk, ch), F32),
            pltpu.VMEM((4, X, 8 * Z, ch), BF16),
            pltpu.VMEM((4, X - 1, 8 * Z, ch), BF16),
            pltpu.VMEM((ch // 128, 8 * Z, 128), F32),
            pltpu.VMEM((4, Z, 8, ch), F32),
            pltpu.VMEM((4, Z - 1, 8, ch), F32),
            pltpu.VMEM((chunk, 128), F32),
            pltpu.VMEM((X - 1, chunk, 128), F32),
            pltpu.VMEM((span, Y, chunk, cols), BF16),
            pltpu.VMEM((CORES * Y, per, chunk, cols), BF16),
            dma,
            dma((span + lead, Y)),
            dma((per, 2)),
            dma((per + Y,)),
            dma((per, Y)),
            dma((per, Y)),
            dma((CORES * Y - 1,)),
            dma((CORES * Y - 1,)),
            dma((Z - 1,)),
            dma((X,)),
            dma((4, X - 1)),
            dma((4, X - 1)),
            dma((4, Z - 1)),
            dma((4, Z - 1)),
            dma((X - 1,)),
            dma((X - 1,)),
            dma((CORES * Y - 1,)),
            dma((CORES * Y - 1,)),
            dma,
            dma,
            pltpu.SemaphoreType.REGULAR,
        ],
        compiler_params=pltpu.CompilerParams(
            collective_id=0, has_side_effects=True, vmem_limit_bytes=60 * 1024 * 1024
        ),
    )(
        clip_frames,
        acts.reshape(per, cols, ch),
        cot.reshape(per, cols, ch),
        weight.transpose(1, 0, 2).reshape(taps, Y, Z, ch),
        centre,
        spread,
        gain.reshape(1, ch),
        bias.reshape(1, ch),
    )
    return grad_input.reshape(1, per, 1, cols, ch), weight_grad


def solution(mesh):
    X, Y, Z = mesh.shape["tm"] // CORES, mesh.shape["height"], mesh.shape["dp"]
    return jax.shard_map(
        functools.partial(per_device, X, Y, Z),
        mesh=mesh,
        in_specs=(
            P("dp", "tm", "height", None, None),
            P("dp", "tm", "height", None, None),
            P("dp"),
            P("dp", None, None),
            P("dp", None),
            P("dp", None),
            P(),
            P(),
        ),
        out_specs=(P("dp", "tm", "height", None, None), P(("tm", "height", "dp"), None)),
        check_vma=False,
    )
```

time: 56.2 us -> 52.6 us (0.936)
  Pallas kernels: 52.1 us -> 48.9 us
    pallas_call x1, Pallas kernels: 52.1 us -> 48.9 us  [per_device(): pl.pallas_call(functools.partial(fused, X, Y, Z), out_shape=(jax.ShapeDty...]
    unnamed x15 -> x4, local copies, waits for them, and re-layouts: 2.64 us -> 2.28 us
where the time goes in v2:
time: 52.6 us; the launch traced here: 52.5 us
  Pallas kernels  48.9 us (93%)
  local copies, waits for them, and re-layouts  2.28 us (4%)
  between operations  1.29 us (2%)
    pallas_call x1, Pallas kernels, per_device(): pl.pallas_call(functools.partial(fused, X, Y, Z), out_shape=(jax.ShapeDty...  48.9 us
    unnamed x4, local copies, waits for them, and re-layouts  2.28 us

profile of v2, /device:TPU:1, one launch (start us, length us, event | category | flops | bytes accessed | tf_op | source)
XLA Modules:
  0.0 52.5 jit_solution(6515170014639156360)
XLA Ops:
  1.3 48.9 %shard_map.95 = (bf16[2,256,256]{2,1,0:T(8,128)(2,1)}, bf16[27,256]{1,0:T(8,128)(2,1)}) custom-call(s32[1]{0:T(128)S(6)} %copy.13.clip_frames, bf16[2,256,256]{2,1,0:T(8,128)(2,1)} %bitcast.12, bf16[2,256,256]{2,1,0:T(8,128)(2,1)} %bitcast.13, bf16[27,4,8,256]{3,2,1,0:T(8,128)(2,1)} %bitcast.10, f32[1,32]{1,0:T(1,128)} %centre.1, f32[1,32]{1,0:T(1,128)} %spread.1, ...), custom_call_target="tpu_custom_call" | custom-call | tf_op jit(solution)/shard_map/pallas_call | solution.py:497
  50.2 0.0 copy-start
  50.2 1.7 %copy.14 = bf16[1,2,1,256,256]{4,3,2,1,0:T(8,128)(2,1)} copy(bf16[1,2,1,256,256]{4,3,2,1,0:T(8,128)(2,1)} %bitcast.11) | data formatting | bytes 524288
  51.9 0.0 copy-done
  51.9 0.6 %copy.15 = bf16[27,256]{1,0:T(8,128)(2,1)} copy(bf16[27,256]{1,0:T(8,128)(2,1)S(1)} %copy-done) | data formatting | bytes 27648
Async XLA Ops:
  50.2 1.7 %copy-start = (bf16[27,256]{1,0:T(8,128)(2,1)S(1)}, bf16[27,256]{1,0:T(8,128)(2,1)}, u32[]{:S(2)}) copy-start(bf16[27,256]{1,0:T(8,128)(2,1)} %get-tuple-element.11) | copy-start | bytes 41476

commit v3 on v2

--- a/solution.py
+++ b/solution.py
@@ -30,8 +30,8 @@
     X, Y, Z,
     clip_frames, acts, cot, weight, centre, spread, gain, bias,
     out, wout,
-    act_in, act_send, act_all, cots, w_all, w_taps, lhs, grad, normed, slope,
-    total, x_send, x_recv, row_sum, z_send, z_recv, s_send, s_recv, g_send, g_recv,
+    act_in, act_send, act_mid, act_all, cots, w_all, w_taps, lhs, grad, normed, slope,
+    total, x_send, x_recv, row_sum, z_send, z_recv, s_send, s_recv, g_send, g_mid, g_recv,
     act_sem, cot_sem, own_send, fwd_send, sis_send, halo_send, a_snd, a_rcv, w_snd, w_rcv,
     x_snd, x_rcv, z_snd, z_rcv, s_snd, s_rcv, g_snd, g_rcv, p_snd, p_rcv, z_ready,
 ):
@@ -65,21 +65,10 @@
         pltpu.make_async_copy(cot.at[k], cots.at[PER * c + k, y], cot_sem.at[PER * c + k, y]).start()
 
     barrier = pltpu.get_barrier_semaphore()
-    partners = [
-        dev(x, (c + dc) % CORES, (y + dy) % Y, z)
-        for dc in range(CORES) for dy in range(Y) if dc or dy
-    ]
+    partners = [sister] + [dev(x, c, (y + dy) % Y, z) for dy in range(1, Y)]
     partners += [dev((x + dx) % X, c, y, z) for dx in range(1, X)]
     for target in partners:
         pl.semaphore_signal(barrier, inc=1, device_id=target, device_id_type=MESH)
-
-    @pl.when(c == 0)
-    def _():
-        pl.semaphore_signal(barrier, inc=1, device_id=dev(prev_x, 1, y, z), device_id_type=MESH)
-
-    @pl.when(c == 1)
-    def _():
-        pl.semaphore_signal(barrier, inc=1, device_id=dev(next_x, 0, y, z), device_id_type=MESH)
 
     for d in range(1, Z):
         @pl.when(z + d < Z)
@@ -101,19 +90,17 @@
     for k in range(PER):
         act_send[:, k] = nt(pick, act_in[k]).astype(BF16).reshape(CORES * Y, chunk, cols)
 
-    pl.semaphore_wait(barrier, len(partners) + 1 + z)
+    pl.semaphore_wait(barrier, len(partners) + z)
 
     def cot_to(k, row, target, snd):
         src = cot.at[k] if row is None else cots.at[PER * c + k, row]
         at = y if row is None else row
         return remote(src, cots.at[PER * c + k, at], snd, cot_sem.at[PER * c + k, at], target)
 
-    def halo_to(k, row, slot):
-        src = cot.at[k] if row is None else cots.at[PER * c + k, row]
-        at = y if row is None else row
+    def halo_to(row, slot):
         return remote(
-            src, cots.at[span + k, at], halo_send.at[k, slot], cot_sem.at[span + k, at],
-            dev(prev_x, k, y, z),
+            cots.at[c, row], cots.at[span + c, row], halo_send.at[slot], cot_sem.at[span + c, row],
+            dev(prev_x, c, y, z),
         )
 
     sends = []
@@ -122,25 +109,34 @@
         copy.start()
         sends.append(copy)
 
-    around = [(dc, dy) for dc in range(CORES) for dy in range(Y) if dc or dy]
-    for n, (dc, dy) in enumerate(around):
-        cc, yy = (c + dc) % CORES, (y + dy) % Y
-        go(remote(
-            act_send.at[cc * Y + yy], act_all.at[pl.ds(lead + PER * c, PER), y], a_snd.at[n], a_rcv.at[n],
-            dev(x, cc, yy, z),
-        ))
-    act_all[pl.ds(lead + PER * c, PER), y] = act_send[c * Y + y]
-
+    def arrived(f, row):
+        remote(
+            cots.at[f, row], cots.at[f, row], own_send.at[0, 0], cot_sem.at[f, row], sister
+        ).wait_recv()
+
+    def blocks_to(n, src, core, dy):
+        return remote(
+            src, act_all.at[pl.ds(lead + PER * core, PER), y], a_snd.at[n], a_rcv.at[n],
+            dev(x, c, (y + dy) % Y, z),
+        )
+
+    go(remote(
+        act_send.at[pl.ds((1 - c) * Y, Y)], act_mid, a_snd.at[0], a_rcv.at[0], sister
+    ))
+    for k in range(PER):
+        go(cot_to(k, None, sister, sis_send.at[k, 0]))
+    for dy in range(1, Y):
+        go(blocks_to(dy, act_send.at[c * Y + (y + dy) % Y], c, dy))
     for k in range(PER):
         ends = (up, down) if k == 0 else (down, up)
         for n, row in enumerate(ends):
             go(cot_to(k, None, dev(x, c, row, z), own_send.at[k, n]))
-    for k in range(PER):
-        go(cot_to(k, None, sister, sis_send.at[k, 0]))
-
-        @pl.when(c == 0)
-        def _():
-            halo_to(k, None, 0).start()
+    act_all[pl.ds(lead + PER * c, PER), y] = act_send[c * Y + y]
+    mid = remote(act_mid, act_mid, a_snd.at[0], a_rcv.at[0], sister)
+    mid.wait_recv()
+    for dy in range(1, Y):
+        go(blocks_to(Y - 1 + dy, act_mid.at[(y + dy) % Y], 1 - c, dy))
+    act_all[pl.ds(lead + PER * (1 - c), PER), y] = act_mid[y]
 
     for d in range(1, Z):
         @pl.when(z >= d)
@@ -179,17 +175,24 @@
     lax.fori_loop(0, span + lead, clear_edges, 0)
     total[...] = jnp.zeros(total.shape, F32)
 
-    def arrived(f, row):
-        remote(
-            cots.at[f, row], cots.at[f, row], own_send.at[0, 0], cot_sem.at[f, row], sister
-        ).wait_recv()
-
-    for n, (dc, dy) in enumerate(around):
-        cs, ys = (c + dc) % CORES, (y + Y - dy) % Y
-        remote(
-            act_send.at[0], act_all.at[pl.ds(lead + PER * cs, PER), ys], a_snd.at[n], a_rcv.at[n], sister
-        ).wait_recv()
-
+    for k in range(PER):
+        arrived(PER * c + k, y)
+
+    def halo_late(row, slot):
+        @pl.when(c == 1)
+        def _():
+            arrived(1, row)
+            halo_to(row, slot).start()
+
+    @pl.when(c == 0)
+    def _():
+        halo_to(y, 0).start()
+
+    halo_late(y, 0)
+    for dy in range(1, Y):
+        for n, core in ((dy, c), (Y - 1 + dy, 1 - c)):
+            blocks = act_all.at[pl.ds(lead + PER * core, PER), (y + Y - dy) % Y]
+            remote(blocks, blocks, a_snd.at[n], a_rcv.at[n], sister).wait_recv()
     go(remote(
         act_all.at[pl.ds(span, lead)], act_all.at[pl.ds(0, lead)], p_snd, p_rcv, dev(next_x, c, y, z)
     ))
@@ -249,7 +252,7 @@
 
     def weight_row(r):
         def body(f, _):
-            @pl.when(c != f // PER)
+            @pl.when((c != f // PER) & ((c == 0) | (f != 1)))
             def _():
                 arrived(f, r)
 
@@ -313,9 +316,10 @@
         seen[k] += 1
         go(cot_to(k, row, sister, sis_send.at[k, n]))
 
-        @pl.when(c == 0)
-        def _():
-            halo_to(k, row, n).start()
+        if k == 0:
+            @pl.when(c == 0)
+            def _():
+                halo_to(row, n).start()
 
     take(0, down, up)
     take(0, up, None)
@@ -335,8 +339,8 @@
     lax.fori_loop(0, lead * Y, prepare_before, 0)
     take(1, up, down)
     take(1, down, None)
-    for k in range(PER):
-        arrived(PER * c + k, y)
+    halo_late(down, 1)
+    halo_late(up, 2)
 
     def turn(n):
         return (y + n + (n // 2) * (1 - 2 * (n % 2))) % Y
@@ -358,12 +362,11 @@
     halo_on(0)
     take(0, across, None)
     take(1, across, None)
+    halo_late(across, 3)
     weight_row(across)
     row_sum[...] = jnp.zeros(row_sum.shape, F32)
     for j in range(len(parts)):
         reduce_x(j)
-    halo_on(1)
-    halo_on(3)
 
     for n in range(X):
         pltpu.make_async_copy(w_all.at[:, n], w_all.at[:, n], w_rcv.at[n]).wait()
@@ -385,22 +388,14 @@
         for f in range(span):
             input_term(f, r)
 
-    for n in range(Y - 1):
+    def input_rows(n, _):
         input_row(turn(n))
-        reduce_z(n)
-    reduce_z(3)
-    halo_on(2)
-    input_row(across)
-    for f in range(span, span + lead):
-        def halo_input(r, _):
-            @pl.when(c != f - span)
-            def _():
-                arrived(f, r)
-
-            input_term(f, r)
-            return 0
-
-        lax.fori_loop(0, Y, halo_input, 0)
+        return 0
+
+    lax.fori_loop(0, 2, input_rows, 0)
+    halo_on(1)
+    halo_on(3)
+    lax.fori_loop(2, Y, input_rows, 0)
 
     def gather(t, carry):
         first, second = carry
@@ -417,7 +412,19 @@
         return first + upstream, second + upstream * normed[s, r]
 
     nothing = jnp.zeros((chunk, cols), F32)
-    first, second = lax.fori_loop(0, span * Y, gather, (nothing, nothing))
+    early_sums = lax.fori_loop(0, (span - lead) * Y, gather, (nothing, nothing))
+    halo_on(2)
+    for f in range(span, span + lead):
+        def halo_input(r, _):
+            @pl.when(c != f - span)
+            def _():
+                arrived(f, r)
+
+            input_term(f, r)
+            return 0
+
+        lax.fori_loop(0, Y, halo_input, 0)
+    first, second = lax.fori_loop((span - lead) * Y, span * Y, gather, early_sums)
     slim = lax.broadcasted_iota(jnp.int32, (chunk, 128), 1)
     first = jnp.sum(first, axis=1, keepdims=True)
     second = jnp.sum(second, axis=1, keepdims=True)
@@ -426,6 +433,9 @@
         go(remote(
             s_send, s_recv.at[d - 1], s_snd.at[d - 1], s_rcv.at[d - 1], dev((x + d) % X, c, y, z)
         ))
+
+    for j in range(len(parts)):
+        reduce_z(j)
 
     for d in range(1, X):
         pltpu.make_async_copy(s_recv.at[d - 1], s_recv.at[d - 1], s_rcv.at[d - 1]).wait()
@@ -438,20 +448,31 @@
     first = jnp.sum(jnp.where(slim == 0, both, 0.0), axis=1, keepdims=True) / population
     second = jnp.sum(jnp.where(slim == 1, both, 0.0), axis=1, keepdims=True) / population
 
-    def finish(t, _):
-        s, r = t // Y, t % Y
-        value = scale * (slope[s, r] - first - normed[s, r] * second) * valid(s)
-        g_send[s, r] = value.astype(BF16)
-        return 0
-
-    lax.fori_loop(0, span * Y, finish, 0)
-    for n, (dc, dy) in enumerate(around):
-        cc, yy = (c + dc) % CORES, (y + dy) % Y
-        go(remote(
-            g_send.at[pl.ds(PER * cc, PER), yy], g_recv.at[c * Y + y], g_snd.at[n], g_rcv.at[n],
-            dev(x, cc, yy, z),
-        ))
+    def finish(core):
+        def body(t, _):
+            s, r = PER * core + t // Y, t % Y
+            value = scale * (slope[s, r] - first - normed[s, r] * second) * valid(s)
+            g_send[s, r] = value.astype(BF16)
+            return 0
+
+        lax.fori_loop(0, PER * Y, body, 0)
+
+    finish(1 - c)
+    go(remote(g_send.at[pl.ds(PER * (1 - c), PER)], g_mid, g_snd.at[0], g_rcv.at[0], sister))
+    finish(c)
+
+    def rows_to(n, src, core, dy):
+        return remote(
+            src, g_recv.at[core * Y + y], g_snd.at[n], g_rcv.at[n], dev(x, c, (y + dy) % Y, z)
+        )
+
+    for dy in range(1, Y):
+        go(rows_to(dy, g_send.at[pl.ds(PER * c, PER), (y + dy) % Y], c, dy))
     g_recv[c * Y + y] = g_send[pl.ds(PER * c, PER), y]
+    remote(g_mid, g_mid, g_snd.at[0], g_rcv.at[0], sister).wait_recv()
+    for dy in range(1, Y):
+        go(rows_to(Y - 1 + dy, g_mid.at[:, (y + dy) % Y], 1 - c, dy))
+    g_recv[(1 - c) * Y + y] = g_mid[:, y]
 
     final = z_send[:, z]
     for j in range(len(parts)):
@@ -463,22 +484,18 @@
     cells = X * Y * Z * CORES * PER * cols
     wout[...] = (final * (1.0 / cells)).astype(BF16)
 
-    for n, (dc, dy) in enumerate(around):
-        cs, ys = (c + dc) % CORES, (y + Y - dy) % Y
-        remote(
-            g_send.at[pl.ds(0, PER), 0], g_recv.at[cs * Y + ys], g_snd.at[n], g_rcv.at[n], sister
-        ).wait_recv()
+    for dy in range(1, Y):
+        for n, core in ((dy, c), (Y - 1 + dy, 1 - c)):
+            rows = g_recv.at[core * Y + (y + Y - dy) % Y]
+            remote(rows, rows, g_snd.at[n], g_rcv.at[n], sister).wait_recv()
     for k in range(PER):
         out[k] = tn(g_recv[:, k].reshape(ch, cols), pick).astype(BF16)
 
     for copy in sends:
         copy.wait_send()
 
-    @pl.when(c == 0)
-    def _():
-        for k in range(PER):
-            for n in range(Y):
-                halo_to(k, y, n).wait_send()
+    for n in range(Y):
+        halo_to(y, n).wait_send()
 
     @pl.when(mine)
     def _():
@@ -505,6 +522,7 @@
         scratch_shapes=[
             pltpu.VMEM((per, cols, ch), BF16),
             pltpu.VMEM((CORES * Y, per, chunk, cols), BF16),
+            pltpu.VMEM((Y, per, chunk, cols), BF16),
             pltpu.VMEM((span + lead, Y, chunk, cols), BF16),
             pltpu.VMEM((span + lead, Y, cols, ch), BF16),
             pltpu.VMEM((taps, X, Z, ch), BF16),
@@ -522,13 +540,14 @@
             pltpu.VMEM((chunk, 128), F32),
             pltpu.VMEM((X - 1, chunk, 128), F32),
             pltpu.VMEM((span, Y, chunk, cols), BF16),
+            pltpu.VMEM((per, Y, chunk, cols), BF16),
             pltpu.VMEM((CORES * Y, per, chunk, cols), BF16),
             dma,
             dma((span + lead, Y)),
             dma((per, 2)),
             dma((per + Y,)),
             dma((per, Y)),
-            dma((per, Y)),
+            dma((Y,)),
             dma((CORES * Y - 1,)),
             dma((CORES * Y - 1,)),
             dma((Z - 1,)),

time: 52.6 us -> 55.4 us (1.053)
  Pallas kernels: 48.9 us -> 51.7 us
    pallas_call x1, Pallas kernels: 48.9 us -> 51.7 us  [per_device(): pl.pallas_call(functools.partial(fused, X, Y, Z), out_shape=(jax.ShapeDty...]
where the time goes in v3:
time: 55.4 us; the launch traced here: 55.2 us
  Pallas kernels  51.7 us (93%)
  local copies, waits for them, and re-layouts  2.28 us (4%)
  between operations  1.29 us (2%)
    pallas_call x1, Pallas kernels, per_device(): pl.pallas_call(functools.partial(fused, X, Y, Z), out_shape=(jax.ShapeDty...  51.7 us
    unnamed x4, local copies, waits for them, and re-layouts  2.28 us

profile of v3, /device:TPU:1, one launch (start us, length us, event | category | flops | bytes accessed | tf_op | source)
XLA Modules:
  0.0 55.2 jit_solution(6880854122348624981)
XLA Ops:
  1.3 51.7 %shard_map.95 = (bf16[2,256,256]{2,1,0:T(8,128)(2,1)}, bf16[27,256]{1,0:T(8,128)(2,1)}) custom-call(s32[1]{0:T(128)S(6)} %copy.13.clip_frames, bf16[2,256,256]{2,1,0:T(8,128)(2,1)} %bitcast.12, bf16[2,256,256]{2,1,0:T(8,128)(2,1)} %bitcast.13, bf16[27,4,8,256]{3,2,1,0:T(8,128)(2,1)} %bitcast.10, f32[1,32]{1,0:T(1,128)} %centre.1, f32[1,32]{1,0:T(1,128)} %spread.1, ...), custom_call_target="tpu_custom_call" | custom-call | tf_op jit(solution)/shard_map/pallas_call | solution.py:514
  53.0 0.0 copy-start
  53.0 1.7 %copy.14 = bf16[1,2,1,256,256]{4,3,2,1,0:T(8,128)(2,1)} copy(bf16[1,2,1,256,256]{4,3,2,1,0:T(8,128)(2,1)} %bitcast.11) | data formatting | bytes 524288
  54.6 0.0 copy-done
  54.6 0.6 %copy.15 = bf16[27,256]{1,0:T(8,128)(2,1)} copy(bf16[27,256]{1,0:T(8,128)(2,1)S(1)} %copy-done) | data formatting | bytes 27648
Async XLA Ops:
  53.0 1.7 %copy-start = (bf16[27,256]{1,0:T(8,128)(2,1)S(1)}, bf16[27,256]{1,0:T(8,128)(2,1)}, u32[]{:S(2)}) copy-start(bf16[27,256]{1,0:T(8,128)(2,1)} %get-tuple-element.11) | copy-start | bytes 41476

commit v4 on v3

--- a/solution.py
+++ b/solution.py
@@ -120,6 +120,30 @@
             dev(x, c, (y + dy) % Y, z),
         )
 
+    for d in range(1, Z):
+        @pl.when(z >= d)
+        def _():
+            pl.semaphore_signal(
+                z_ready, inc=1, device_id=dev(x, c, y, (z + Z - d) % Z), device_id_type=MESH
+            )
+
+    mine = (z % CORES) == c
+    wsrc = weight.at[:, y]
+
+    def weight_to(d):
+        return remote(
+            wsrc, w_all.at[:, z // CORES], w_snd.at[d - 1], w_rcv.at[z // CORES],
+            dev(x, c, y, (z + d) % Z),
+        )
+
+    @pl.when(mine)
+    def _():
+        pltpu.make_async_copy(wsrc, w_all.at[:, z // CORES], w_rcv.at[z // CORES]).start()
+        for d in range(1, Z):
+            @pl.when(z + d >= Z)
+            def _():
+                weight_to(d).start()
+
     go(remote(
         act_send.at[pl.ds((1 - c) * Y, Y)], act_mid, a_snd.at[0], a_rcv.at[0], sister
     ))
@@ -127,40 +151,16 @@
         go(cot_to(k, None, sister, sis_send.at[k, 0]))
     for dy in range(1, Y):
         go(blocks_to(dy, act_send.at[c * Y + (y + dy) % Y], c, dy))
-    for k in range(PER):
-        ends = (up, down) if k == 0 else (down, up)
-        for n, row in enumerate(ends):
-            go(cot_to(k, None, dev(x, c, row, z), own_send.at[k, n]))
     act_all[pl.ds(lead + PER * c, PER), y] = act_send[c * Y + y]
     mid = remote(act_mid, act_mid, a_snd.at[0], a_rcv.at[0], sister)
     mid.wait_recv()
     for dy in range(1, Y):
         go(blocks_to(Y - 1 + dy, act_mid.at[(y + dy) % Y], 1 - c, dy))
+    for k in range(PER):
+        ends = (up, down) if k == 0 else (down, up)
+        for n, row in enumerate(ends):
+            go(cot_to(k, None, dev(x, c, row, z), own_send.at[k, n]))
     act_all[pl.ds(lead + PER * (1 - c), PER), y] = act_mid[y]
-
-    for d in range(1, Z):
-        @pl.when(z >= d)
-        def _():
-            pl.semaphore_signal(
-                z_ready, inc=1, device_id=dev(x, c, y, (z + Z - d) % Z), device_id_type=MESH
-            )
-
-    mine = (z % CORES) == c
-    wsrc = weight.at[:, y]
-
-    def weight_to(d):
-        return remote(
-            wsrc, w_all.at[:, z // CORES], w_snd.at[d - 1], w_rcv.at[z // CORES],
-            dev(x, c, y, (z + d) % Z),
-        )
-
-    @pl.when(mine)
-    def _():
-        pltpu.make_async_copy(wsrc, w_all.at[:, z // CORES], w_rcv.at[z // CORES]).start()
-        for d in range(1, Z):
-            @pl.when(z + d >= Z)
-            def _():
-                weight_to(d).start()
 
     def clear(s, _):
         grad[s] = jnp.zeros(grad.shape[1:], F32)
@@ -240,27 +240,23 @@
         block_input(t // Y - lead, t % Y)
         return 0
 
-    lax.fori_loop(0, span * Y, prepare, 0)
+    lax.fori_loop(0, span * Y, prepare, 0, unroll=2)
 
     rows3 = lhs.shape[2]
-
-    def taps_of(f):
-        return max(0, lead - f), min(3, span + lead - f)
 
     def masked(f, r):
         return jnp.where(x * span + f < clip_len, cots[f, r], jnp.zeros((cols, ch), BF16))
 
     def weight_row(r):
-        def body(f, _):
+        for f in range(span):
             @pl.when((c != f // PER) & ((c == 0) | (f != 1)))
             def _():
                 arrived(f, r)
 
-            left = lhs[pl.ds(f, 3), pl.ds(r, 3)].reshape(9 * rows3, cols)
-            total[pl.ds(0, 27)] += nn(left, masked(f, r)).reshape(27, chunk, ch)
-            return 0
-
-        lax.fori_loop(0, span, body, 0)
+        left = [lhs[pl.ds(f, 3), pl.ds(r, 3)].reshape(9 * rows3, cols) for f in range(span)]
+        right = [masked(f, r) for f in range(span)]
+        term = nn(jnp.concatenate(left, axis=1), jnp.concatenate(right, axis=0))
+        total[...] += term.reshape(27, chunk, ch)
 
     parts = [(t, min(8, 27 - t)) for t in range(0, 27, 8)]
 
@@ -336,7 +332,7 @@
                 weight_to(d).start()
 
     pltpu.make_async_copy(act_all.at[pl.ds(0, lead)], act_all.at[pl.ds(0, lead)], p_rcv).wait()
-    lax.fori_loop(0, lead * Y, prepare_before, 0)
+    lax.fori_loop(0, lead * Y, prepare_before, 0, unroll=2)
     take(1, up, down)
     take(1, down, None)
     halo_late(down, 1)
@@ -371,26 +367,30 @@
     for n in range(X):
         pltpu.make_async_copy(w_all.at[:, n], w_all.at[:, n], w_rcv.at[n]).wait()
 
-    def by_tap(k, _):
+    for k in range(9):
         tap = w_all[pl.ds(3 * k, 3)].astype(F32).reshape(rows3, ch)
-        w_taps[k // 3, k % 3] = tap.astype(BF16)
+        w_taps[pl.ds(k % 3 * rows3, rows3), pl.ds((2 - k // 3) * ch, ch)] = tap.astype(BF16)
+
+    def input_term(s, f0, f1, r):
+        k0, k1 = (f0 - s) * ch, (f1 - s) * ch
+        right = jnp.concatenate([masked(f, r) for f in range(f0, f1)], axis=1)
+        part = nt(w_taps[:, pl.ds(k0, k1 - k0)], right)
+        grad[s, pl.ds(r, 3)] += part.reshape(3, rows3, cols)
+
+    def input_rows(n, _):
+        for s in range(span):
+            input_term(s, s, min(s + 3, span), turn(n))
         return 0
 
-    lax.fori_loop(0, 9, by_tap, 0)
-
-    def input_term(f, r):
-        k0, k1 = taps_of(f)
-        s0, n = f - lead + k0, k1 - k0
-        left = w_taps[pl.ds(k0, n)].reshape(n * 3 * rows3, ch)
-        grad[pl.ds(s0, n), pl.ds(r, 3)] += nt(left, masked(f, r)).reshape(n, 3, rows3, cols)
-
-    def input_row(r):
-        for f in range(span):
-            input_term(f, r)
-
-    def input_rows(n, _):
-        input_row(turn(n))
-        return 0
+    def halo_input(d):
+        r = (y + d) % Y
+        for f in range(span, span + lead):
+            @pl.when(c != f - span)
+            def _():
+                arrived(f, r)
+
+        for s in range(span - lead, span):
+            input_term(s, span, s + 3, r)
 
     lax.fori_loop(0, 2, input_rows, 0)
     halo_on(1)
@@ -412,19 +412,14 @@
         return first + upstream, second + upstream * normed[s, r]
 
     nothing = jnp.zeros((chunk, cols), F32)
-    early_sums = lax.fori_loop(0, (span - lead) * Y, gather, (nothing, nothing))
+    early_sums = lax.fori_loop(0, (span - lead) * Y, gather, (nothing, nothing), unroll=2)
+    for d in (0, 1, 3):
+        halo_input(d)
+    reduce_z(0)
     halo_on(2)
-    for f in range(span, span + lead):
-        def halo_input(r, _):
-            @pl.when(c != f - span)
-            def _():
-                arrived(f, r)
-
-            input_term(f, r)
-            return 0
-
-        lax.fori_loop(0, Y, halo_input, 0)
-    first, second = lax.fori_loop((span - lead) * Y, span * Y, gather, early_sums)
+    reduce_z(1)
+    halo_input(2)
+    first, second = lax.fori_loop((span - lead) * Y, span * Y, gather, early_sums, unroll=2)
     slim = lax.broadcasted_iota(jnp.int32, (chunk, 128), 1)
     first = jnp.sum(first, axis=1, keepdims=True)
     second = jnp.sum(second, axis=1, keepdims=True)
@@ -434,8 +429,8 @@
             s_send, s_recv.at[d - 1], s_snd.at[d - 1], s_rcv.at[d - 1], dev((x + d) % X, c, y, z)
         ))
 
-    for j in range(len(parts)):
-        reduce_z(j)
+    reduce_z(2)
+    reduce_z(3)
 
     for d in range(1, X):
         pltpu.make_async_copy(s_recv.at[d - 1], s_recv.at[d - 1], s_rcv.at[d - 1]).wait()
@@ -455,7 +450,7 @@
             g_send[s, r] = value.astype(BF16)
             return 0
 
-        lax.fori_loop(0, PER * Y, body, 0)
+        lax.fori_loop(0, PER * Y, body, 0, unroll=4)
 
     finish(1 - c)
     go(remote(g_send.at[pl.ds(PER * (1 - c), PER)], g_mid, g_snd.at[0], g_rcv.at[0], sister))
@@ -526,7 +521,7 @@
             pltpu.VMEM((span + lead, Y, chunk, cols), BF16),
             pltpu.VMEM((span + lead, Y, cols, ch), BF16),
             pltpu.VMEM((taps, X, Z, ch), BF16),
-            pltpu.VMEM((3, 3, 3 * chunk, ch), BF16),
+            pltpu.VMEM((9 * chunk, 3 * ch), BF16),
             pltpu.VMEM((span + lead, Y + 2, 3 * chunk, cols), BF16),
             pltpu.VMEM((span, Y + 2, 3 * chunk, cols), F32),
             pltpu.VMEM((span, Y, chunk, cols), F32),

time: 55.4 us -> 48.6 us (0.88)
  Pallas kernels: 51.7 us -> 44.8 us
    pallas_call x1, Pallas kernels: 51.7 us -> 44.8 us  [per_device(): pl.pallas_call(functools.partial(fused, X, Y, Z), out_shape=(jax.ShapeDty...]
where the time goes in v4:
time: 48.6 us; the launch traced here: 48.4 us
  Pallas kernels  44.8 us (92%)
  local copies, waits for them, and re-layouts  2.28 us (5%)
  between operations  1.29 us (3%)
    pallas_call x1, Pallas kernels, per_device(): pl.pallas_call(functools.partial(fused, X, Y, Z), out_shape=(jax.ShapeDty...  44.8 us
    unnamed x4, local copies, waits for them, and re-layouts  2.28 us

profile of v4, /device:TPU:1, one launch (start us, length us, event | category | flops | bytes accessed | tf_op | source)
XLA Modules:
  0.0 48.4 jit_solution(4481728552228021462)
XLA Ops:
  1.3 44.8 %shard_map.95 = (bf16[2,256,256]{2,1,0:T(8,128)(2,1)}, bf16[27,256]{1,0:T(8,128)(2,1)}) custom-call(s32[1]{0:T(128)S(6)} %copy.13.clip_frames, bf16[2,256,256]{2,1,0:T(8,128)(2,1)} %bitcast.12, bf16[2,256,256]{2,1,0:T(8,128)(2,1)} %bitcast.13, bf16[27,4,8,256]{3,2,1,0:T(8,128)(2,1)} %bitcast.10, f32[1,32]{1,0:T(1,128)} %centre.1, f32[1,32]{1,0:T(1,128)} %spread.1, ...), custom_call_target="tpu_custom_call" | custom-call | tf_op jit(solution)/shard_map/pallas_call | solution.py:509
  46.1 0.0 copy-start
  46.1 1.7 %copy.14 = bf16[1,2,1,256,256]{4,3,2,1,0:T(8,128)(2,1)} copy(bf16[1,2,1,256,256]{4,3,2,1,0:T(8,128)(2,1)} %bitcast.11) | data formatting | bytes 524288
  47.8 0.0 copy-done
  47.8 0.6 %copy.15 = bf16[27,256]{1,0:T(8,128)(2,1)} copy(bf16[27,256]{1,0:T(8,128)(2,1)S(1)} %copy-done) | data formatting | bytes 27648
Async XLA Ops:
  46.1 1.7 %copy-start = (bf16[27,256]{1,0:T(8,128)(2,1)S(1)}, bf16[27,256]{1,0:T(8,128)(2,1)}, u32[]{:S(2)}) copy-start(bf16[27,256]{1,0:T(8,128)(2,1)} %get-tuple-element.11) | copy-start | bytes 41476

commit v5 on v4

--- a/solution.py
+++ b/solution.py
@@ -560,7 +560,7 @@
             pltpu.SemaphoreType.REGULAR,
         ],
         compiler_params=pltpu.CompilerParams(
-            collective_id=0, has_side_effects=True, vmem_limit_bytes=60 * 1024 * 1024
+            collective_id=0, has_side_effects=True, vmem_limit_bytes=54784 * 1024
         ),
     )(
         clip_frames,

time: 48.6 us -> 46.9 us (0.965)
  Pallas kernels: 44.8 us -> 43.5 us
    pallas_call x1, Pallas kernels: 44.8 us -> 43.5 us  [per_device(): pl.pallas_call(functools.partial(fused, X, Y, Z), out_shape=(jax.ShapeDty...]
    unnamed x4 -> x10, local copies, waits for them, and re-layouts: 2.28 us -> 1.99 us
where the time goes in v5:
time: 46.9 us; the launch traced here: 46.8 us
  Pallas kernels  43.5 us (93%)
  local copies, waits for them, and re-layouts  1.99 us (4%)
  between operations  1.32 us (3%)
    pallas_call x1, Pallas kernels, per_device(): pl.pallas_call(functools.partial(fused, X, Y, Z), out_shape=(jax.ShapeDty...  43.5 us
    unnamed x10, local copies, waits for them, and re-layouts  1.99 us

profile of v5, /device:TPU:1, one launch (start us, length us, event | category | flops | bytes accessed | tf_op | source)
XLA Modules:
  0.0 46.8 jit_solution(2230179822564228991)
XLA Ops:
  1.3 0.0 copy-start.1
  1.3 0.0 copy-start.3
  1.3 0.0 copy-start
  1.3 0.0 copy-start.2
  1.3 0.6 %copy-done.1 = f32[256]{0:T(256)S(1)} copy-done((f32[256]{0:T(256)S(1)}, f32[256]{0:T(256)}, u32[]{:S(2)}) %copy-start.1) | copy-done | bytes 1048
  2.0 0.0 copy-done.3
  2.0 0.0 copy-done
  2.0 0.0 copy-done.2
  2.0 43.5 %shard_map.95 = (bf16[2,256,256]{2,1,0:T(8,128)(2,1)S(1)}, bf16[27,256]{1,0:T(8,128)(2,1)S(1)}) custom-call(s32[1]{0:T(128)S(6)} %copy.13.clip_frames, bf16[2,256,256]{2,1,0:T(8,128)(2,1)} %bitcast.14, bf16[2,256,256]{2,1,0:T(8,128)(2,1)} %bitcast.15, bf16[27,4,8,256]{3,2,1,0:T(8,128)(2,1)} %bitcast.13, f32[1,32]{1,0:T(1,128)S(1)} %copy-done.2, ...), custom_call_target="tpu_custom_call" | custom-call | tf_op jit(solution)/shard_map/pallas_call | solution.py:509
  45.5 0.7 %copy.14 = bf16[1,2,1,256,256]{4,3,2,1,0:T(8,128)(2,1)} copy(bf16[1,2,1,256,256]{4,3,2,1,0:T(8,128)(2,1)S(1)} %bitcast.10) | data formatting | bytes 524288
  46.2 0.6 %copy.15 = bf16[27,256]{1,0:T(8,128)(2,1)} copy(bf16[27,256]{1,0:T(8,128)(2,1)S(1)} %get-tuple-element.11) | data formatting | bytes 27648
Async XLA Ops:
  1.3 0.7 %copy-start.1 = (f32[256]{0:T(256)S(1)}, f32[256]{0:T(256)}, u32[]{:S(2)}) copy-start(f32[256]{0:T(256)} %param.15) | copy-start | bytes 3076
  1.3 0.7 %copy-start.3 = (f32[1,32]{1,0:T(1,128)S(1)}, f32[1,32]{1,0:T(1,128)}, u32[]{:S(2)}) copy-start(f32[1,32]{1,0:T(1,128)} %spread.1) | copy-start | bytes 388
  1.3 0.7 %copy-start = (f32[256]{0:T(256)S(1)}, f32[256]{0:T(256)}, u32[]{:S(2)}) copy-start(f32[256]{0:T(256)} %param.14) | copy-start | bytes 3076
  1.3 0.7 %copy-start.2 = (f32[1,32]{1,0:T(1,128)S(1)}, f32[1,32]{1,0:T(1,128)}, u32[]{:S(2)}) copy-start(f32[1,32]{1,0:T(1,128)} %centre.1) | copy-start | bytes 388

commit v6 on v5

--- a/solution.py
+++ b/solution.py
@@ -240,7 +240,7 @@
         block_input(t // Y - lead, t % Y)
         return 0
 
-    lax.fori_loop(0, span * Y, prepare, 0, unroll=2)
+    lax.fori_loop(0, span * Y, prepare, 0, unroll=4)
 
     rows3 = lhs.shape[2]
 
@@ -412,14 +412,14 @@
         return first + upstream, second + upstream * normed[s, r]
 
     nothing = jnp.zeros((chunk, cols), F32)
-    early_sums = lax.fori_loop(0, (span - lead) * Y, gather, (nothing, nothing), unroll=2)
+    early_sums = lax.fori_loop(0, (span - lead) * Y, gather, (nothing, nothing), unroll=4)
     for d in (0, 1, 3):
         halo_input(d)
     reduce_z(0)
     halo_on(2)
     reduce_z(1)
     halo_input(2)
-    first, second = lax.fori_loop((span - lead) * Y, span * Y, gather, early_sums, unroll=2)
+    first, second = lax.fori_loop((span - lead) * Y, span * Y, gather, early_sums, unroll=8)
     slim = lax.broadcasted_iota(jnp.int32, (chunk, 128), 1)
     first = jnp.sum(first, axis=1, keepdims=True)
     second = jnp.sum(second, axis=1, keepdims=True)
@@ -450,19 +450,18 @@
             g_send[s, r] = value.astype(BF16)
             return 0
 
-        lax.fori_loop(0, PER * Y, body, 0, unroll=4)
-
-    finish(1 - c)
-    go(remote(g_send.at[pl.ds(PER * (1 - c), PER)], g_mid, g_snd.at[0], g_rcv.at[0], sister))
-    finish(c)
+        lax.fori_loop(0, PER * Y, body, 0, unroll=8)
 
     def rows_to(n, src, core, dy):
         return remote(
             src, g_recv.at[core * Y + y], g_snd.at[n], g_rcv.at[n], dev(x, c, (y + dy) % Y, z)
         )
 
+    finish(c)
     for dy in range(1, Y):
         go(rows_to(dy, g_send.at[pl.ds(PER * c, PER), (y + dy) % Y], c, dy))
+    finish(1 - c)
+    go(remote(g_send.at[pl.ds(PER * (1 - c), PER)], g_mid, g_snd.at[0], g_rcv.at[0], sister))
     g_recv[c * Y + y] = g_send[pl.ds(PER * c, PER), y]
     remote(g_mid, g_mid, g_snd.at[0], g_rcv.at[0], sister).wait_recv()
     for dy in range(1, Y):

time: 46.9 us -> 46.6 us (level)
  no operation moved by 1% of the time
where the time goes in v6:
time: 46.6 us; the launch traced here: 46.5 us
  Pallas kernels  43.2 us (93%)
  local copies, waits for them, and re-layouts  1.99 us (4%)
  between operations  1.32 us (3%)
    pallas_call x1, Pallas kernels, per_device(): pl.pallas_call(functools.partial(fused, X, Y, Z), out_shape=(jax.ShapeDty...  43.2 us
    unnamed x10, local copies, waits for them, and re-layouts  1.99 us

profile of v6, /device:TPU:1, one launch (start us, length us, event | category | flops | bytes accessed | tf_op | source)
XLA Modules:
  0.0 46.5 jit_solution(7089125248731226378)
XLA Ops:
  1.3 0.0 copy-start.1
  1.3 0.0 copy-start.3
  1.3 0.0 copy-start
  1.3 0.0 copy-start.2
  1.3 0.6 %copy-done.1 = f32[256]{0:T(256)S(1)} copy-done((f32[256]{0:T(256)S(1)}, f32[256]{0:T(256)}, u32[]{:S(2)}) %copy-start.1) | copy-done | bytes 1048
  2.0 0.0 copy-done.3
  2.0 0.0 copy-done
  2.0 0.0 copy-done.2
  2.0 43.2 %shard_map.95 = (bf16[2,256,256]{2,1,0:T(8,128)(2,1)S(1)}, bf16[27,256]{1,0:T(8,128)(2,1)S(1)}) custom-call(s32[1]{0:T(128)S(6)} %copy.13.clip_frames, bf16[2,256,256]{2,1,0:T(8,128)(2,1)} %bitcast.14, bf16[2,256,256]{2,1,0:T(8,128)(2,1)} %bitcast.15, bf16[27,4,8,256]{3,2,1,0:T(8,128)(2,1)} %bitcast.13, f32[1,32]{1,0:T(1,128)S(1)} %copy-done.2, ...), custom_call_target="tpu_custom_call" | custom-call | tf_op jit(solution)/shard_map/pallas_call | solution.py:508
  45.2 0.7 %copy.14 = bf16[1,2,1,256,256]{4,3,2,1,0:T(8,128)(2,1)} copy(bf16[1,2,1,256,256]{4,3,2,1,0:T(8,128)(2,1)S(1)} %bitcast.10) | data formatting | bytes 524288
  45.9 0.6 %copy.15 = bf16[27,256]{1,0:T(8,128)(2,1)} copy(bf16[27,256]{1,0:T(8,128)(2,1)S(1)} %get-tuple-element.11) | data formatting | bytes 27648
Async XLA Ops:
  1.3 0.7 %copy-start.1 = (f32[256]{0:T(256)S(1)}, f32[256]{0:T(256)}, u32[]{:S(2)}) copy-start(f32[256]{0:T(256)} %param.15) | copy-start | bytes 3076
  1.3 0.7 %copy-start.3 = (f32[1,32]{1,0:T(1,128)S(1)}, f32[1,32]{1,0:T(1,128)}, u32[]{:S(2)}) copy-start(f32[1,32]{1,0:T(1,128)} %spread.1) | copy-start | bytes 388
  1.3 0.7 %copy-start = (f32[256]{0:T(256)S(1)}, f32[256]{0:T(256)}, u32[]{:S(2)}) copy-start(f32[256]{0:T(256)} %param.14) | copy-start | bytes 3076
  1.3 0.7 %copy-start.2 = (f32[1,32]{1,0:T(1,128)S(1)}, f32[1,32]{1,0:T(1,128)}, u32[]{:S(2)}) copy-start(f32[1,32]{1,0:T(1,128)} %centre.1) | copy-start | bytes 388

commit v7 on v6

--- a/solution.py
+++ b/solution.py
@@ -245,6 +245,8 @@
     rows3 = lhs.shape[2]
 
     def masked(f, r):
+        if f < span - 1:
+            return cots[f, r]
         return jnp.where(x * span + f < clip_len, cots[f, r], jnp.zeros((cols, ch), BF16))
 
     def weight_row(r):

time: 46.6 us -> 46.7 us (level)
  no operation moved by 1% of the time
where the time goes in v7:
time: 46.7 us; the launch traced here: 46.6 us
  Pallas kernels  43.2 us (93%)
  local copies, waits for them, and re-layouts  1.99 us (4%)
  between operations  1.32 us (3%)
    pallas_call x1, Pallas kernels, per_device(): pl.pallas_call(functools.partial(fused, X, Y, Z), out_shape=(jax.ShapeDty...  43.2 us
    unnamed x10, local copies, waits for them, and re-layouts  1.99 us

profile of v7, /device:TPU:1, one launch (start us, length us, event | category | flops | bytes accessed | tf_op | source)
XLA Modules:
  0.0 46.6 jit_solution(12309955830004016337)
XLA Ops:
  1.3 0.0 copy-start.1
  1.3 0.0 copy-start.3
  1.3 0.0 copy-start
  1.3 0.0 copy-start.2
  1.3 0.6 %copy-done.1 = f32[256]{0:T(256)S(1)} copy-done((f32[256]{0:T(256)S(1)}, f32[256]{0:T(256)}, u32[]{:S(2)}) %copy-start.1) | copy-done | bytes 1048
  2.0 0.0 copy-done.3
  2.0 0.0 copy-done
  2.0 0.0 copy-done.2
  2.0 43.2 %shard_map.95 = (bf16[2,256,256]{2,1,0:T(8,128)(2,1)S(1)}, bf16[27,256]{1,0:T(8,128)(2,1)S(1)}) custom-call(s32[1]{0:T(128)S(6)} %copy.13.clip_frames, bf16[2,256,256]{2,1,0:T(8,128)(2,1)} %bitcast.14, bf16[2,256,256]{2,1,0:T(8,128)(2,1)} %bitcast.15, bf16[27,4,8,256]{3,2,1,0:T(8,128)(2,1)} %bitcast.13, f32[1,32]{1,0:T(1,128)S(1)} %copy-done.2, ...), custom_call_target="tpu_custom_call" | custom-call | tf_op jit(solution)/shard_map/pallas_call | solution.py:510
  45.2 0.7 %copy.14 = bf16[1,2,1,256,256]{4,3,2,1,0:T(8,128)(2,1)} copy(bf16[1,2,1,256,256]{4,3,2,1,0:T(8,128)(2,1)S(1)} %bitcast.10) | data formatting | bytes 524288
  45.9 0.6 %copy.15 = bf16[27,256]{1,0:T(8,128)(2,1)} copy(bf16[27,256]{1,0:T(8,128)(2,1)S(1)} %get-tuple-element.11) | data formatting | bytes 27648
Async XLA Ops:
  1.3 0.7 %copy-start.1 = (f32[256]{0:T(256)S(1)}, f32[256]{0:T(256)}, u32[]{:S(2)}) copy-start(f32[256]{0:T(256)} %param.15) | copy-start | bytes 3076
  1.3 0.7 %copy-start.3 = (f32[1,32]{1,0:T(1,128)S(1)}, f32[1,32]{1,0:T(1,128)}, u32[]{:S(2)}) copy-start(f32[1,32]{1,0:T(1,128)} %spread.1) | copy-start | bytes 388
  1.3 0.7 %copy-start = (f32[256]{0:T(256)S(1)}, f32[256]{0:T(256)}, u32[]{:S(2)}) copy-start(f32[256]{0:T(256)} %param.14) | copy-start | bytes 3076
  1.3 0.7 %copy-start.2 = (f32[1,32]{1,0:T(1,128)S(1)}, f32[1,32]{1,0:T(1,128)}, u32[]{:S(2)}) copy-start(f32[1,32]{1,0:T(1,128)} %centre.1) | copy-start | bytes 388
